TPU v7x, 32 devices: a whole 2x2x4 slice. The times are simulated.
32 devices in a mesh: grp: 2 (over x), pulse: 16 (over z, y, core).
Axes of the slice: x: 2, y: 2, z: 4, core: 2. Of those that a mesh axis runs over, the one named last changes fastest.
Arguments:
- echo: float32 [2, 4, 4, 2048, 1024], P(None, 'grp', None, 'pulse'), parts along dimension 1, may hold values from -6 to 6
- spectral_shift_units: int32 [1024], replicated, may hold values from -256 to 256
Outputs:
- doppler: float32 [2, 4, 4, 1024, 2048], P(None, 'grp', None, 'pulse'), parts along dimension 1
There are 2 independent parts, one for each index of `grp`. A program takes and returns all parts, laid end to end along the dimension named above; an argument that names none is the same for every part. Nothing has to cross between parts.
Inputs may be any that keep to these rules, and one draw needn't show every extreme that they name: `spectral_shift_units`: bin codes may repeat.
All inputs are finite; a program needn't handle non-finite values.
Results may differ from a plain program's by a relative error of at most 0.00007.
Values sent between devices are 32-bit elements; how exact they have to be, the bound alone decides.
No kernel may reach another device: no remote copies, remote signals or barrier semaphores. Data moves between devices by JAX's collectives and lax.ppermute only.
A program may use at most 192 MiB of HBM per device.

v0:
```python
import math

import jax
import jax.numpy as jnp
from jax import lax
from jax.sharding import PartitionSpec as P

PULSES = 2048


BETA_KB = math.pi * math.sqrt(35.2)


def bessel_zero(value):
    quarter = value * value * 0.25
    term = jnp.ones_like(value)
    total = jnp.ones_like(value)
    for order in range(1, 41):
        term = term * quarter / float(order * order)
        total = total + term
    return total


def kernel(distance):
    ratio = distance / 4.0
    inner = jnp.maximum(1.0 - ratio * ratio, 0.0)
    peak = bessel_zero(BETA_KB * jnp.ones((), distance.dtype))
    return bessel_zero(BETA_KB * jnp.sqrt(inner)) / peak


def positions(spectral_shift_units, echo_numbers, number_of_echoes):
    center_tone_hertz = 16 * number_of_echoes
    quotient_numerator = 2 * (echo_numbers[None, :] - number_of_echoes // 2) * center_tone_hertz
    quotient_denominator = center_tone_hertz + spectral_shift_units[:, None]
    cell_floor = jnp.floor_divide(quotient_numerator, quotient_denominator)
    fraction = (quotient_numerator - cell_floor * quotient_denominator).astype(
        jnp.float32
    ) / quotient_denominator.astype(jnp.float32)
    return (cell_floor, fraction)


def correction(number_of_echoes):
    grid_size = 2 * number_of_echoes
    doppler_bin_index = jnp.arange(number_of_echoes, dtype=jnp.int32) - number_of_echoes // 2
    phase = math.pi * 8.0 / grid_size * doppler_bin_index.astype(jnp.float32)
    root = jnp.sqrt(BETA_KB * BETA_KB - phase * phase)
    parity = (1 - 2 * (doppler_bin_index % 2)).astype(jnp.float32)
    peak = bessel_zero(BETA_KB * jnp.ones((), jnp.float32))
    return parity * peak * root / (8.0 * jnp.sinh(root)) / math.sqrt(number_of_echoes)


def localize(cell_floor, anchor, number_of_echoes, slack):
    grid_size = 2 * number_of_echoes
    return (cell_floor + number_of_echoes - anchor + slack) % grid_size - slack


def spread(samples, local_cells, fraction, width):
    number_of_keys = local_cells.shape[0]
    block_rows = min(128, number_of_keys)
    cell_ids = jnp.arange(width, dtype=jnp.int32)
    tap_offsets = jnp.arange(8, dtype=jnp.int32) - 3
    tap_weight = kernel(tap_offsets.astype(jnp.float32)[None, None, :] - fraction[:, :, None])

    def one_block(block_id):
        start = block_id * block_rows
        rel_cells = lax.dynamic_slice_in_dim(local_cells, start, block_rows, 0)
        rel_taps = lax.dynamic_slice_in_dim(tap_weight, start, block_rows, 0)
        displacement = cell_ids[None, None, :] - rel_cells[:, :, None]
        weight = jnp.zeros(displacement.shape, jnp.float32)
        for tap_index in range(8):
            weight = jnp.where(
                displacement == tap_index - 3, rel_taps[:, :, tap_index : tap_index + 1], weight
            )
        segment = lax.dynamic_slice_in_dim(samples, start, block_rows, 4)
        return jnp.einsum("zcypk,kpw->zcykw", segment, weight, precision=lax.Precision.HIGHEST)

    blocks = lax.map(one_block, jnp.arange(number_of_keys // block_rows, dtype=jnp.int32))
    blocks = jnp.moveaxis(blocks, 0, 3)
    lead_shape = blocks.shape[:3]
    return blocks.reshape(lead_shape + (number_of_keys, width))


def rotate(real_part, imag_part, cosine, sine, form):
    highest = lax.Precision.HIGHEST
    new_real = jnp.einsum(form, real_part, cosine, precision=highest) + jnp.einsum(
        form, imag_part, sine, precision=highest
    )
    new_imag = jnp.einsum(form, imag_part, cosine, precision=highest) - jnp.einsum(
        form, real_part, sine, precision=highest
    )
    return (new_real, new_imag)


def transform(gridded, number_of_echoes):
    grid_size = 2 * number_of_echoes
    outer_len = math.gcd(grid_size, 2 ** ((grid_size.bit_length() - 1) // 2))
    inner_len = grid_size // outer_len
    lead_shape = gridded.shape[1:-1]
    real_part = gridded[0].reshape(lead_shape + (outer_len, inner_len))
    imag_part = gridded[1].reshape(lead_shape + (outer_len, inner_len))
    outer_ids = jnp.arange(outer_len, dtype=jnp.int32)
    inner_ids = jnp.arange(inner_len, dtype=jnp.int32)
    first_phase = (
        2.0
        * math.pi
        / outer_len
        * (outer_ids[:, None] * outer_ids[None, :] % outer_len).astype(jnp.float32)
    )
    mid_real, mid_imag = rotate(
        real_part, imag_part, jnp.cos(first_phase), jnp.sin(first_phase), "...ab,an->...nb"
    )
    twist = (
        2.0
        * math.pi
        / grid_size
        * (outer_ids[:, None] * inner_ids[None, :] % grid_size).astype(jnp.float32)
    )
    twist_cos = jnp.cos(twist)
    twist_sin = jnp.sin(twist)
    turned_real = mid_real * twist_cos + mid_imag * twist_sin
    turned_imag = mid_imag * twist_cos - mid_real * twist_sin
    last_phase = (
        2.0
        * math.pi
        / inner_len
        * (inner_ids[:, None] * inner_ids[None, :] % inner_len).astype(jnp.float32)
    )
    out_real, out_imag = rotate(
        turned_real, turned_imag, jnp.cos(last_phase), jnp.sin(last_phase), "...nb,bm->...mn"
    )
    out_real = out_real.reshape(lead_shape + (grid_size,))
    out_imag = out_imag.reshape(lead_shape + (grid_size,))
    half_count = number_of_echoes // 2
    picked_real = jnp.concatenate(
        [out_real[..., grid_size - half_count :], out_real[..., :half_count]], axis=-1
    )
    picked_imag = jnp.concatenate(
        [out_imag[..., grid_size - half_count :], out_imag[..., :half_count]], axis=-1
    )
    scaling = correction(number_of_echoes)
    return jnp.stack([picked_real * scaling, picked_imag * scaling])


def on_device(echo, spectral_shift_units):
    number_of_echoes = PULSES
    grid_size = 2 * number_of_echoes
    per_device = echo.shape[3]
    device_pos = lax.axis_index("pulse")
    rim_cells = number_of_echoes // 128 + 8
    moved = lax.all_to_all(echo, "pulse", split_axis=4, concat_axis=3, tiled=True)
    own_bins = moved.shape[4]
    codes = lax.dynamic_slice_in_dim(spectral_shift_units, device_pos * own_bins, own_bins, 0)
    tile_count = number_of_echoes // per_device
    cell_floor, fraction = positions(
        codes, jnp.arange(number_of_echoes, dtype=jnp.int32), number_of_echoes
    )
    anchors = jnp.repeat(
        jnp.arange(tile_count, dtype=jnp.int32) * (2 * per_device) - rim_cells, per_device
    )
    local_cells = localize(cell_floor, anchors[None, :], number_of_echoes, rim_cells)
    local_cells = local_cells.reshape(own_bins * tile_count, per_device)
    fraction = fraction.reshape(own_bins * tile_count, per_device)
    lead_shape = moved.shape[:3]
    samples = moved.reshape(lead_shape + (tile_count, per_device, own_bins))
    samples = jnp.transpose(samples, (0, 1, 2, 4, 5, 3)).reshape(
        lead_shape + (per_device, own_bins * tile_count)
    )
    width = 2 * per_device + 2 * rim_cells
    extended = spread(samples, local_cells, fraction, width)
    extended = extended.reshape(lead_shape + (own_bins, tile_count, width))
    middle = extended[..., rim_cells : rim_cells + 2 * per_device]
    left_parts = jnp.roll(extended[..., :rim_cells], -1, axis=4)
    right_parts = jnp.roll(extended[..., rim_cells + 2 * per_device :], 1, axis=4)
    middle = middle.at[..., 2 * per_device - rim_cells :].add(left_parts)
    middle = middle.at[..., :rim_cells].add(right_parts)
    gridded = middle.reshape(lead_shape + (own_bins, grid_size))
    return transform(gridded, number_of_echoes)


def solution(mesh):
    placed = (P(None, "grp", None, "pulse", None), P())
    return jax.shard_map(
        on_device,
        mesh=mesh,
        in_specs=placed,
        out_specs=P(None, "grp", None, "pulse", None),
        check_vma=False,
    )
```

profile of v0, /device:TPU:15, one launch (start us, length us, event | category | flops | bytes accessed | tf_op | source)
XLA Modules:
  0.0 1184.7 jit_solution(13333686495005674387)
XLA Ops:
  0.0 10.2 copy.53
  10.2 6.6 all-to-all-start
  19.8 5.5 fusion.72
  25.3 5.5 fusion.75
  31.4 20.1 %add_multiply_fusion = f32[1024,128,8]{1,0,2:T(8,128)} fusion(f32[1024,128]{1,0:T(8,128)S(1)} %fusion.75, f32[8]{0:T(128)S(1)} %add_convert_fusion), kind=kLoop, calls=%fused_computation.77 | loop fusion | flops 133169152 | bytes 4718624 | tf_op jit(solution)/shard_map/div | solution.py:28
  51.5 147.6 %all-to-all-done = f32[2,2,4,128,1024]{3,2,1,0,4:T(4,128)} async-done(((f32[2,2,4,128,1024]{3,2,1,0,4:T(4,128)}), f32[2,2,4,128,1024]{3,2,1,0,4:T(4,128)}, u32[]{:S(2)}, u32[]{:S(2)}) %all-to-all-start) | async-done | bytes 8388640 | tf_op jit(solution)/shard_map/all_to_all | solution.py:150
  199.1 6.1 copy.54
  205.2 9.9 copy.55
  215.1 297.3 %while.13 = (s32[]{:T(128)}, f32[8,2,2,4,128,304]{5,4,0,3,2,1:T(8,128)}, s32[8]{0:T(128)S(1)}, s32[1024,128]{1,0:T(8,128)S(1)}, f32[1024,128,8]{1,0,2:T(8,128)},...) while((s32[]{:T(128)}, ...), condition=%wide.region_1.2_spmd.clone, body=%wide.region_0.1_spmd.clone.sunk | while | flops 1040973824 | bytes 13042015 | solution.py:77
  216.8 1.1 dynamic-slice_bitcast_fusion.9
  217.9 1.3 constant_dynamic-slice_fusion.5
  219.3 30.7 %fusion.172 = f32[1,2,2,4,128,304]{5,3,2,1,4,0:T(4,128)S(1)} fusion(f32[128,128]{1,0:T(8,128)S(1)} %get-tuple-element.188, f32[128,128]{1,0:T(8,128)S(1)} %get-tuple-element.189, f32[128,128]{1,0:T(8,128)S(1)} %get-tuple-element.190, f32[128,128]{1,0:T(8,128)S(1)} %get-tuple-element.191, f32[128,128]{1,0:T(8,128)S(1)} %get-tuple-element.192, ...), kind=kOutput, calls=%fused_computation.39.clone.1 | convolution fusion | flops 1040973824 | bytes 4128768 | tf_op jit(solution)/shard_map/while/body/eval_jaxpr/zcypk,kpw->zcykw/dot_general | solution.py:75
  250.0 2.7 copy_dynamic-update-slice_fusion.2
  253.9 1.1 dynamic-slice_bitcast_fusion.9
  255.0 1.3 constant_dynamic-slice_fusion.5
  256.4 30.7 %fusion.172 = f32[1,2,2,4,128,304]{5,3,2,1,4,0:T(4,128)S(1)} fusion(f32[128,128]{1,0:T(8,128)S(1)} %get-tuple-element.188, f32[128,128]{1,0:T(8,128)S(1)} %get-tuple-element.189, f32[128,128]{1,0:T(8,128)S(1)} %get-tuple-element.190, f32[128,128]{1,0:T(8,128)S(1)} %get-tuple-element.191, f32[128,128]{1,0:T(8,128)S(1)} %get-tuple-element.192, ...), kind=kOutput, calls=%fused_computation.39.clone.1 | convolution fusion | flops 1040973824 | bytes 4128768 | tf_op jit(solution)/shard_map/while/body/eval_jaxpr/zcypk,kpw->zcykw/dot_general | solution.py:75
  287.1 2.7 copy_dynamic-update-slice_fusion.2
  291.0 1.1 dynamic-slice_bitcast_fusion.9
  292.2 1.3 constant_dynamic-slice_fusion.5
  293.5 30.7 %fusion.172 = f32[1,2,2,4,128,304]{5,3,2,1,4,0:T(4,128)S(1)} fusion(f32[128,128]{1,0:T(8,128)S(1)} %get-tuple-element.188, f32[128,128]{1,0:T(8,128)S(1)} %get-tuple-element.189, f32[128,128]{1,0:T(8,128)S(1)} %get-tuple-element.190, f32[128,128]{1,0:T(8,128)S(1)} %get-tuple-element.191, f32[128,128]{1,0:T(8,128)S(1)} %get-tuple-element.192, ...), kind=kOutput, calls=%fused_computation.39.clone.1 | convolution fusion | flops 1040973824 | bytes 4128768 | tf_op jit(solution)/shard_map/while/body/eval_jaxpr/zcypk,kpw->zcykw/dot_general | solution.py:75
  324.2 2.6 copy_dynamic-update-slice_fusion.2
  329.2 1.3 constant_dynamic-slice_fusion.5
  330.6 30.7 %fusion.172 = f32[1,2,2,4,128,304]{5,3,2,1,4,0:T(4,128)S(1)} fusion(f32[128,128]{1,0:T(8,128)S(1)} %get-tuple-element.188, f32[128,128]{1,0:T(8,128)S(1)} %get-tuple-element.189, f32[128,128]{1,0:T(8,128)S(1)} %get-tuple-element.190, f32[128,128]{1,0:T(8,128)S(1)} %get-tuple-element.191, f32[128,128]{1,0:T(8,128)S(1)} %get-tuple-element.192, ...), kind=kOutput, calls=%fused_computation.39.clone.1 | convolution fusion | flops 1040973824 | bytes 4128768 | tf_op jit(solution)/shard_map/while/body/eval_jaxpr/zcypk,kpw->zcykw/dot_general | solution.py:75
  361.3 2.7 copy_dynamic-update-slice_fusion.2
  365.2 1.1 dynamic-slice_bitcast_fusion.9
  366.3 1.3 constant_dynamic-slice_fusion.5
  367.7 30.7 %fusion.172 = f32[1,2,2,4,128,304]{5,3,2,1,4,0:T(4,128)S(1)} fusion(f32[128,128]{1,0:T(8,128)S(1)} %get-tuple-element.188, f32[128,128]{1,0:T(8,128)S(1)} %get-tuple-element.189, f32[128,128]{1,0:T(8,128)S(1)} %get-tuple-element.190, f32[128,128]{1,0:T(8,128)S(1)} %get-tuple-element.191, f32[128,128]{1,0:T(8,128)S(1)} %get-tuple-element.192, ...), kind=kOutput, calls=%fused_computation.39.clone.1 | convolution fusion | flops 1040973824 | bytes 4128768 | tf_op jit(solution)/shard_map/while/body/eval_jaxpr/zcypk,kpw->zcykw/dot_general | solution.py:75
  398.4 2.6 copy_dynamic-update-slice_fusion.2
  402.3 1.1 dynamic-slice_bitcast_fusion.9
  403.4 1.3 constant_dynamic-slice_fusion.5
  404.7 30.7 %fusion.172 = f32[1,2,2,4,128,304]{5,3,2,1,4,0:T(4,128)S(1)} fusion(f32[128,128]{1,0:T(8,128)S(1)} %get-tuple-element.188, f32[128,128]{1,0:T(8,128)S(1)} %get-tuple-element.189, f32[128,128]{1,0:T(8,128)S(1)} %get-tuple-element.190, f32[128,128]{1,0:T(8,128)S(1)} %get-tuple-element.191, f32[128,128]{1,0:T(8,128)S(1)} %get-tuple-element.192, ...), kind=kOutput, calls=%fused_computation.39.clone.1 | convolution fusion | flops 1040973824 | bytes 4128768 | tf_op jit(solution)/shard_map/while/body/eval_jaxpr/zcypk,kpw->zcykw/dot_general | solution.py:75
  435.5 2.6 copy_dynamic-update-slice_fusion.2
  439.4 1.1 dynamic-slice_bitcast_fusion.9
  440.5 1.3 constant_dynamic-slice_fusion.5
  441.8 30.7 %fusion.172 = f32[1,2,2,4,128,304]{5,3,2,1,4,0:T(4,128)S(1)} fusion(f32[128,128]{1,0:T(8,128)S(1)} %get-tuple-element.188, f32[128,128]{1,0:T(8,128)S(1)} %get-tuple-element.189, f32[128,128]{1,0:T(8,128)S(1)} %get-tuple-element.190, f32[128,128]{1,0:T(8,128)S(1)} %get-tuple-element.191, f32[128,128]{1,0:T(8,128)S(1)} %get-tuple-element.192, ...), kind=kOutput, calls=%fused_computation.39.clone.1 | convolution fusion | flops 1040973824 | bytes 4128768 | tf_op jit(solution)/shard_map/while/body/eval_jaxpr/zcypk,kpw->zcykw/dot_general | solution.py:75
  472.6 2.6 copy_dynamic-update-slice_fusion.2
  476.4 1.1 dynamic-slice_bitcast_fusion.9
  477.6 1.3 constant_dynamic-slice_fusion.5
  478.9 30.7 %fusion.172 = f32[1,2,2,4,128,304]{5,3,2,1,4,0:T(4,128)S(1)} fusion(f32[128,128]{1,0:T(8,128)S(1)} %get-tuple-element.188, f32[128,128]{1,0:T(8,128)S(1)} %get-tuple-element.189, f32[128,128]{1,0:T(8,128)S(1)} %get-tuple-element.190, f32[128,128]{1,0:T(8,128)S(1)} %get-tuple-element.191, f32[128,128]{1,0:T(8,128)S(1)} %get-tuple-element.192, ...), kind=kOutput, calls=%fused_computation.39.clone.1 | convolution fusion | flops 1040973824 | bytes 4128768 | tf_op jit(solution)/shard_map/while/body/eval_jaxpr/zcypk,kpw->zcykw/dot_general | solution.py:75
  509.6 2.7 copy_dynamic-update-slice_fusion.2
  512.5 14.5 %slice.169 = f32[2,2,4,64,16,256]{5,4,3,2,1,0:T(8,128)} slice(f32[2,2,4,64,16,304]{5,4,3,2,1,0:T(8,128)} %bitcast.133), slice={[0:2], [0:2], [0:4], [0:64], [0:16], [24:280]} | slice | bytes 33554432 | tf_op jit(solution)/shard_map/slice | solution.py:171
  527.0 5.1 fusion.160
  532.1 9.5 fusion.161
  541.7 6.4 slice_add_fusion.1
  548.0 168.2 %scatter-add.6 = f32[2,2,4,64,16,256]{5,4,3,2,1,0:T(8,128)} dynamic-update-slice(f32[2,2,4,64,16,256]{5,4,3,2,1,0:T(8,128)} %slice.169, f32[2,2,4,64,16,24]{5,4,3,2,1,0:T(8,128)} %slice_add_fusion.1, s32[]{:T(128)} %constant.253.clone.1, s32[]{:T(128)} %constant.253.clone.1, s32[]{:T(128)} %constant.253.clone.1, s32[]{:T(128)} %constant.253.clone.1, s32[]{:T(128)} %constant.253.clone.1, ...) | dynamic-update-slice | bytes 3145732 | tf_op jit(solution)/shard_map/scatter-add | solution.py:174
  716.2 9.9 slice_add_fusion
  726.1 48.4 %scatter-add.9 = f32[2,2,4,64,16,256]{5,4,3,2,1,0:T(8,128)} dynamic-update-slice(f32[2,2,4,64,16,256]{5,4,3,2,1,0:T(8,128)} %scatter-add.6, f32[2,2,4,64,16,24]{5,4,3,2,1,0:T(8,128)} %slice_add_fusion, s32[]{:T(128)} %constant.253.clone.1, s32[]{:T(128)} %constant.253.clone.1, s32[]{:T(128)} %constant.253.clone.1, s32[]{:T(128)} %constant.253.clone.1, s32[]{:T(128)} %constant.253.clone.1, ...) | dynamic-update-slice | bytes 3145732 | tf_op jit(solution)/shard_map/scatter-add | solution.py:175
  774.5 10.9 fusion.162
  785.5 12.7 %reshape_squeeze.6 = f32[2,4,64,64,64]{4,3,2,1,0:T(8,128)} reshape(f32[1,2,4,64,16,256]{5,4,3,2,1,0:T(8,128)} %get-tuple-element.133) | data formatting | bytes 16777216 | tf_op jit(solution)/shard_map/reshape;squeeze | solution.py:99
  798.2 21.9 %fusion.83 = f32[64,2,4,64,64]{4,0,3,2,1:T(8,128)} fusion(f32[2,4,64,64,64]{4,3,2,1,0:T(8,128)} %reshape_squeeze.6), kind=kOutput, calls=%fused_computation.107 | convolution fusion | flops 1610670080 | bytes 16777216 | tf_op jit(solution)/shard_map/...ab,an->...nb/dot_general | solution.py:88
  820.1 22.1 %fusion.91 = f32[64,2,4,64,64]{4,0,3,2,1:T(8,128)} fusion(f32[2,4,64,64,64]{4,3,2,1,0:T(8,128)} %reshape_squeeze.6), kind=kOutput, calls=%fused_computation.115 | convolution fusion | flops 1610670080 | bytes 16777216 | tf_op jit(solution)/shard_map/...ab,an->...nb/dot_general | solution.py:85
  842.2 12.7 %reshape_squeeze.7 = f32[2,4,64,64,64]{4,3,2,1,0:T(8,128)} reshape(f32[1,2,4,64,16,256]{5,4,3,2,1,0:T(8,128)} %get-tuple-element.134) | data formatting | bytes 16777216 | tf_op jit(solution)/shard_map/reshape;squeeze | solution.py:100
  854.9 21.9 %fusion.85 = f32[64,2,4,64,64]{4,0,3,2,1:T(8,128)} fusion(f32[2,4,64,64,64]{4,3,2,1,0:T(8,128)} %reshape_squeeze.7), kind=kOutput, calls=%fused_computation.109 | convolution fusion | flops 1610670080 | bytes 16777216 | tf_op jit(solution)/shard_map/...ab,an->...nb/dot_general | solution.py:85
  876.8 36.3 %multiply_add_fusion = (f32[64,2,4,64,64]{4,0,3,2,1:T(8,128)}, f32[64,2,4,64,64]{4,0,3,2,1:T(8,128)}) fusion(f32[64,64]{1,0:T(8,128)S(1)} %copy-done.1, f32[64,64]{1,0:T(8,128)S(1)} %copy-done.2, f32[64,2,4,64,64]{4,0,3,2,1:T(8,128)} %fusion.83, f32[64,2,4,64,64]{4,0,3,2,1:T(8,128)} %fusion.91, f32[64,2,4,64,64]{4,0,3,2,1:T(8,128)} %fusion.85, ...), kind=kOutput, calls=%fused_computation.71 | convolution fusion | flops 1627447296 | bytes 50364416 | tf_op jit(solution)/shard_map/...ab,an->...nb/dot_general | solution.py:88
  913.2 55.4 %fusion.61 = f32[64,2,4,64,64]{4,0,3,2,1:T(8,128)} fusion(f32[64,2,4,64,64]{4,0,3,2,1:T(8,128)} %get-tuple-element.128), kind=kOutput, calls=%fused_computation.62 | convolution fusion | flops 1610670080 | bytes 16777216 | tf_op jit(solution)/shard_map/...nb,bm->...mn/dot_general | solution.py:85
  968.5 54.8 %fusion.59 = f32[64,2,4,64,64]{4,0,3,2,1:T(8,128)} fusion(f32[64,2,4,64,64]{4,0,3,2,1:T(8,128)} %get-tuple-element.128), kind=kOutput, calls=%fused_computation.60 | convolution fusion | flops 1610670080 | bytes 16777216 | tf_op jit(solution)/shard_map/...nb,bm->...mn/dot_general | solution.py:88
  1023.4 57.6 %add_bitcast_fusion = f32[2,4,64,64,64]{4,3,2,1,0:T(8,128)} fusion(f32[64,2,4,64,64]{4,0,3,2,1:T(8,128)} %fusion.61, f32[64,2,4,64,64]{4,0,3,2,1:T(8,128)} %get-tuple-element.127), kind=kOutput, calls=%fused_computation.69 | convolution fusion | flops 1612767232 | bytes 25165824 | tf_op jit(solution)/shard_map/...nb,bm->...mn/dot_general | solution.py:85
  1081.0 14.7 %reshape.392 = f32[2,4,64,4096]{3,2,1,0:T(8,128)} reshape(f32[2,4,64,64,64]{4,3,2,1,0:T(8,128)} %add_bitcast_fusion) | data formatting | bytes 16777216 | tf_op jit(solution)/shard_map/reshape | solution.py:131
  1095.7 4.0 slice_bitcast_fusion.3
  1099.7 57.6 %subtract_bitcast_fusion = f32[2,4,64,64,64]{4,3,2,1,0:T(8,128)} fusion(f32[64,2,4,64,64]{4,0,3,2,1:T(8,128)} %fusion.59, f32[64,2,4,64,64]{4,0,3,2,1:T(8,128)} %get-tuple-element.127), kind=kOutput, calls=%fused_computation.68 | convolution fusion | flops 1612767232 | bytes 25165824 | tf_op jit(solution)/shard_map/...nb,bm->...mn/dot_general | solution.py:88
  1157.3 14.7 %reshape.393 = f32[2,4,64,4096]{3,2,1,0:T(8,128)} reshape(f32[2,4,64,64,64]{4,3,2,1,0:T(8,128)} %subtract_bitcast_fusion) | data formatting | bytes 16777216 | tf_op jit(solution)/shard_map/reshape | solution.py:132
  1172.0 4.9 slice_bitcast_fusion.1
  1177.0 3.5 maximum_multiply_fusion
  1180.5 4.0 pad_maximum_fusion
  (45 shorter events, 9.7 us)
Async XLA Ops:
  10.2 188.9 %all-to-all-start = ((f32[2,2,4,128,1024]{3,2,1,0,4:T(4,128)}), f32[2,2,4,128,1024]{3,2,1,0,4:T(4,128)}, u32[]{:S(2)}, u32[]{:S(2)}) async-start(f32[2,2,4,128,1024]{3,2,1,0,4:T(4,128)} %copy.53), calls=%async_computation | async-start | bytes 16777216 | tf_op jit(solution)/shard_map/all_to_all | solution.py:150
  854.9 21.9 %copy-start.1 = (f32[64,64]{1,0:T(8,128)S(1)}, f32[64,64]{1,0:T(8,128)}, u32[]{:S(2)}) copy-start(f32[64,64]{1,0:T(8,128)} %copy.59) | copy-start | bytes 49156
  854.9 21.9 %copy-start.2 = (f32[64,64]{1,0:T(8,128)S(1)}, f32[64,64]{1,0:T(8,128)}, u32[]{:S(2)}) copy-start(f32[64,64]{1,0:T(8,128)} %copy.58) | copy-start | bytes 49156
  1172.0 4.9 copy-start
  1172.0 4.9 copy-start.3
where the time goes:
time: 1200 us; the launch traced here: 1180 us
  matrix products  573 us (48%)
  local copies, waits for them, and re-layouts  394 us (33%)
  waiting for transfers between devices  148 us (12%)
  other arithmetic  56.5 us (5%)
    dot_general x8, matrix products, one_block(): jnp.einsum('zcypk,kpw->zcykw', segment, weight, precision=lax.Precision.H...  246 us
    scatter-add x1, local copies, waits for them, and re-layouts, on_device(): middle = middle.at[..., 2 * per_device - rim_cells:].add(left_parts)  168 us
    all_to_all x1, waiting for transfers between devices, on_device(): lax.all_to_all(echo, 'pulse', split_axis=4, concat_axis=3, tiled=True)  148 us
    dot_general x2, matrix products, rotate(): jnp.einsum(form, imag_part, cosine, precision=highest)  91.1 us
    dot_general x2, matrix products, rotate(): jnp.einsum(form, real_part, cosine, precision=highest)  79.7 us
    dot_general x2, matrix products, rotate(): jnp.einsum(form, real_part, sine, precision=highest)  79.5 us
    dot_general x2, matrix products, rotate(): jnp.einsum(form, imag_part, sine, precision=highest)  77.3 us
    scatter-add x1, local copies, waits for them, and re-layouts, on_device(): middle = middle.at[..., :rim_cells].add(right_parts)  48.4 us
  transfers between devices with their start and end apart: 1, of which 1 were waited for; matrix products, arithmetic and copies ran while one was open for 3% of the time, Pallas kernels for 0%

commit v1 on v0

v1 whole, which is shorter than its diff:
```python
import functools
import math

import jax
import jax.numpy as jnp
import numpy as np
from jax import lax
from jax.experimental import pallas as pl
from jax.experimental.pallas import tpu as pltpu
from jax.sharding import PartitionSpec as P

PULSES = 2048
BINS = 1024
TONE = 16 * PULSES
CODE_MAX = PULSES // 8
MINOR = 16
MAJOR = PULSES // MINOR
PAD = 10
BLOCKS = MAJOR // 8
LANES = 128

BETA_KB = math.pi * math.sqrt(35.2)


def bessel_zero(value):
    quarter = value * value * 0.25
    term = jnp.ones_like(value)
    total = jnp.ones_like(value)
    for order in range(1, 41):
        term = term * quarter / float(order * order)
        total = total + term
    return total


def correction(number_of_echoes):
    grid_size = 2 * number_of_echoes
    doppler_bin_index = jnp.arange(number_of_echoes, dtype=jnp.int32) - number_of_echoes // 2
    phase = math.pi * 8.0 / grid_size * doppler_bin_index.astype(jnp.float32)
    root = jnp.sqrt(BETA_KB * BETA_KB - phase * phase)
    parity = (1 - 2 * (doppler_bin_index % 2)).astype(jnp.float32)
    peak = bessel_zero(BETA_KB * jnp.ones((), jnp.float32))
    return parity * peak * root / (8.0 * jnp.sinh(root)) / math.sqrt(number_of_echoes)


@functools.lru_cache(None)
def windows():
    pulse = np.arange(PULSES)
    numerator = 2 * (pulse - PULSES // 2) * TONE
    ends = np.stack([numerator // (TONE + code) - 2 * (pulse - PULSES // 2) for code in (-CODE_MAX, CODE_MAX)])
    low, high = ends.min(0) - 3, ends.max(0) + 4
    out, start = [], 0
    for block in range(BLOCKS):
        row = []
        pairs = np.arange(128 * block, 128 * (block + 1))
        for parity in range(2):
            offsets = []
            for e in range(-PAD, PAD + 1):
                source = (pairs - e) % PULSES
                reach = 2 * e + parity
                if np.any((low[source] <= reach) & (reach <= high[source])):
                    offsets.append(e)
            row.append((start, tuple(offsets)))
            start += len(offsets)
        out.append(tuple(row))
    return tuple(out), start


@functools.lru_cache(None)
def series():
    terms = [1.0]
    for order in range(1, 41):
        terms.append(terms[-1] * (BETA_KB * BETA_KB / 4.0) / float(order * order))
    peak = math.fsum(terms)
    return tuple(term / peak for term in terms)


@functools.lru_cache(None)
def turns():
    r = np.arange(2 * MINOR)[:, None, None]
    n2 = np.arange(MAJOR)[None, :, None]
    q2 = np.arange(MAJOR)[None, None, :]
    angle = 2.0 * math.pi / (2 * PULSES) * ((32 * q2 + r) * n2 % (2 * PULSES))
    cosine, sine = np.cos(angle), np.sin(angle)
    full = np.concatenate(
        [np.concatenate([cosine, sine], 2), np.concatenate([-sine, cosine], 2)], 1
    )
    high = full.astype(jnp.bfloat16)
    low = (full - high.astype(np.float64)).astype(jnp.bfloat16)
    both = np.stack([high, low], 1)
    return both.reshape(MINOR, 2, 2, 2 * MAJOR, 2 * MAJOR)


def pack_body(rows, bins, echo_ref, out_ref):
    depth = echo_ref.shape[2] // MINOR
    lane = lax.broadcasted_iota(jnp.int32, (depth, LANES), 1) // bins
    for part in range(2):
        for m1 in range(MINOR):
            taken = [echo_ref[part, row, pl.ds(m1, depth, stride=MINOR), :] for row in range(rows)]
            for dest in range(rows):
                value = None
                for row in range(rows):
                    turn = (row - dest) * bins % LANES
                    moved = pltpu.roll(taken[row], turn, 1) if turn else taken[row]
                    value = moved if value is None else jnp.where(lane == row, moved, value)
                out_ref[dest, 0, part, pl.ds(m1 * depth, depth), :] = value


def pack(echo, first, count, devices):
    bins = BINS // devices
    rows = LANES // bins
    held = echo.shape[2]
    return pl.pallas_call(
        functools.partial(pack_body, rows, bins),
        grid=(count, BINS // LANES),
        in_specs=[
            pl.BlockSpec((2, rows, held, LANES), lambda u, c: (0, u + first, 0, c)),
        ],
        out_specs=pl.BlockSpec((rows, 1, 2, held, LANES), lambda u, c: (c, u, 0, 0, 0)),
        out_shape=jax.ShapeDtypeStruct((devices, count, 2, held, LANES), jnp.float32),
        cost_estimate=pl.CostEstimate(
            flops=0, bytes_accessed=16 * devices * count * held * LANES, transcendentals=0
        ),
        name="pack",
    )(echo)


def extend(ref, store):
    for m1 in range(MINOR - PAD, MINOR):
        store(m1 - MINOR + PAD, pltpu.roll(ref(m1 + PAD), 1, 0))
    for m1 in range(PAD):
        store(m1 + MINOR + PAD, pltpu.roll(ref(m1 + PAD), MAJOR - 1, 0))


def weight_body(shift_ref, fraction_ref, out_ref, taps, shifts):
    q1 = pl.program_id(0)

    @pl.when(q1 == 0)
    def _():
        coefficients = series()

        @pl.loop(0, MINOR)
        def _(m1):
            shifts[PAD + m1] = shift_ref[m1]

            @pl.loop(0, BLOCKS)
            def _(block):
                at = pl.ds(pl.multiple_of(block * 8, 8), 8)
                fraction = fraction_ref[m1, at, :]
                for tap in range(8):
                    ratio = (float(tap - 3) - fraction) / 4.0
                    inner = jnp.maximum(1.0 - ratio * ratio, 0.0)
                    total = jnp.full_like(inner, coefficients[40])
                    for order in range(39, -1, -1):
                        total = total * inner + coefficients[order]
                    taps[tap, PAD + m1, at, :] = total

        def keep(tap, row, value):
            taps[tap, row] = value

        def keep_shift(row, value):
            shifts[row] = value

        @pl.loop(0, 8)
        def _(tap):
            extend(lambda row: taps[tap, row], functools.partial(keep, tap))

        extend(lambda row: shifts[row], keep_shift)

    table, _ = windows()
    for block in range(BLOCKS):
        at = pl.ds(8 * block, 8)
        for parity in range(2):
            start, offsets = table[block][parity]
            for index, e in enumerate(offsets):
                row = q1 - e + PAD
                shift = shifts[row, at, :]
                value = jnp.zeros((8, LANES), jnp.float32)
                for tap in range(8):
                    value = jnp.where(shift == 2 * e + parity + 3 - tap, taps[tap, row, at, :], value)
                out_ref[0, start + index] = value


def weights(codes):
    _, entries = windows()
    pulse = jnp.arange(MINOR, dtype=jnp.int32)[:, None] + MINOR * jnp.arange(MAJOR, dtype=jnp.int32)[None, :]
    slow = (pulse - PULSES // 2)[:, :, None]
    numerator = 2 * slow * TONE
    denominator = TONE + codes[None, None, :]
    cell_floor = jnp.floor_divide(numerator, denominator)
    fraction = (numerator - cell_floor * denominator).astype(jnp.float32) / denominator.astype(jnp.float32)
    shift = cell_floor - 2 * slow
    whole = pl.BlockSpec((MINOR, MAJOR, LANES), lambda q: (0, 0, 0))
    spread = MINOR + 2 * PAD
    return pl.pallas_call(
        weight_body,
        grid=(MINOR,),
        in_specs=[whole, whole],
        out_specs=pl.BlockSpec((1, entries, 8, LANES), lambda q: (q, 0, 0, 0)),
        out_shape=jax.ShapeDtypeStruct((MINOR, entries, 8, LANES), jnp.float32),
        scratch_shapes=[
            pltpu.VMEM((8, spread, MAJOR, LANES), jnp.float32),
            pltpu.VMEM((spread, MAJOR, LANES), jnp.int32),
        ],
        compiler_params=pltpu.CompilerParams(vmem_limit_bytes=56 * 2**20),
        cost_estimate=pl.CostEstimate(
            flops=100 * 2**20 * 8, bytes_accessed=64 * 2**20, transcendentals=0
        ),
        name="weights",
    )(shift, fraction)


def times(value, turn, size):
    real, imag = value
    turn %= size
    if turn == 0:
        return value
    if 4 * turn == size:
        return (imag, -real)
    if 2 * turn == size:
        return (-real, -imag)
    if 4 * turn == 3 * size:
        return (-imag, real)
    if (8 * turn) % size == 0:
        half = math.sqrt(0.5)
        kind = 8 * turn // size
        if kind == 1:
            return (half * (real + imag), half * (imag - real))
        if kind == 3:
            return (half * (imag - real), -half * (real + imag))
        if kind == 5:
            return (-half * (real + imag), half * (real - imag))
        return (half * (real - imag), half * (real + imag))
    cosine = math.cos(2.0 * math.pi * turn / size)
    sine = math.sin(2.0 * math.pi * turn / size)
    return (real * cosine + imag * sine, imag * cosine - real * sine)


def plus(one, two):
    return (one[0] + two[0], one[1] + two[1])


def minus(one, two):
    return (one[0] - two[0], one[1] - two[1])


def dft4(values):
    sum_a, dif_a = plus(values[0], values[2]), minus(values[0], values[2])
    sum_b, dif_b = plus(values[1], values[3]), minus(values[1], values[3])
    side = (dif_b[1], -dif_b[0])
    return [plus(sum_a, sum_b), plus(dif_a, side), minus(sum_a, sum_b), minus(dif_a, side)]


def dft16(load):
    columns = []
    for low in range(4):
        done = dft4([load(low + 4 * high) for high in range(4)])
        columns.append([times(done[k], low * k, 16) for k in range(4)])
    result = [None] * 16
    for k in range(4):
        done = dft4([columns[low][k] for low in range(4)])
        for high in range(4):
            result[k + 4 * high] = done[high]
    return result


def main_body(first, count, rows, bins, has_base, recv_ref, weight_ref, turn_ref, scale_ref, *rest):
    if has_base:
        rest = rest[1:]
    out_ref, spread, pairs, mids, tall, wide, sem = rest
    q1 = pl.program_id(0)
    devices, depth = recv_ref.shape[0], recv_ref.shape[3] // MINOR

    @pl.when(q1 == 0)
    def _():
        for unit in range(count):
            for part in range(2):
                @pl.loop(0, MINOR)
                def _(m1):
                    for device in range(devices):
                        at = pl.ds(pl.multiple_of(m1 * depth, depth), depth)
                        spread[PAD + m1, part, unit, pl.ds(device * depth, depth), :] = recv_ref[device, unit, part, at, :]

                def keep(row, value):
                    spread[row, part, unit] = value

                extend(lambda row: spread[row, part, unit], keep)

    table, _ = windows()
    for parity in range(2):
        for block in range(BLOCKS):
            start, offsets = table[block][parity]
            sums = [[None] * count, [None] * count]
            for index, e in enumerate(offsets):
                weight = weight_ref[0, start + index]
                row = q1 - e + PAD
                for part in range(2):
                    for unit in range(count):
                        term = weight * spread[row, part, unit, pl.ds(8 * block, 8), :]
                        held = sums[part][unit]
                        sums[part][unit] = term if held is None else held + term
            for part in range(2):
                for unit in range(count):
                    pairs[parity, pl.ds(part * MAJOR + 8 * block, 8), pl.ds(unit * LANES, LANES)] = sums[part][unit]
    for parity in range(2):
        full = pairs[parity]
        high = full.astype(jnp.bfloat16)
        low = (full - high.astype(jnp.float32)).astype(jnp.bfloat16)
        turn_high, turn_low = turn_ref[0, parity, 0], turn_ref[0, parity, 1]
        dot = functools.partial(jnp.dot, preferred_element_type=jnp.float32)
        mids[q1, parity] = dot(turn_high, high) + (dot(turn_high, low) + dot(turn_low, high))

    @pl.when(q1 == MINOR - 1)
    def _():
        for unit in range(count):
            across = pl.ds(unit * LANES, LANES)

            @pl.loop(0, BLOCKS)
            def _(block):
                def load(parity, q):
                    return tuple(
                        mids[q, parity, pl.ds(pl.multiple_of(part * MAJOR + 8 * block, 8), 8), across]
                        for part in range(2)
                    )

                even = dft16(functools.partial(load, 0))
                odd = dft16(functools.partial(load, 1))
                for n1 in range(16):
                    k = n1 - 8
                    value = plus(even[k % 16], times(odd[k % 16], k, 32))
                    for part in range(2):
                        tall[part, n1, pl.ds(pl.multiple_of(8 * block, 8), 8), :] = value[part]

            @pl.loop(0, 16)
            def _(n1):
                at = pl.ds(pl.multiple_of(n1 * LANES, LANES), LANES)
                scale = scale_ref[pl.ds(0, 1), at]
                for part in range(2):
                    turned = jnp.transpose(tall[part, n1]) * scale
                    for row in range(rows):
                        wide[part, unit * rows + row, :, at] = turned[row * bins : (row + 1) * bins]

            copy = pltpu.make_async_copy(
                wide.at[:, pl.ds(unit * rows, rows)],
                out_ref.at[:, pl.ds((first + unit) * rows, rows)],
                sem.at[unit],
            )
            copy.start()
        for unit in range(count):
            pltpu.make_async_copy(
                wide.at[:, pl.ds(unit * rows, rows)],
                out_ref.at[:, pl.ds((first + unit) * rows, rows)],
                sem.at[unit],
            ).wait()


def finish(recv, weight, turn, scale, base, first, total):
    devices, count = recv.shape[0], recv.shape[1]
    bins = BINS // devices
    rows = LANES // bins
    _, entries = windows()
    one = pl.Buffered(1)
    in_specs = [
        pl.BlockSpec(recv.shape, lambda q: (0, 0, 0, 0, 0), pipeline_mode=one),
        pl.BlockSpec((1, entries, 8, LANES), lambda q: (q, 0, 0, 0)),
        pl.BlockSpec((1, 2, 2, 2 * MAJOR, 2 * MAJOR), lambda q: (q, 0, 0, 0, 0)),
        pl.BlockSpec((1, PULSES), lambda q: (0, 0)),
    ]
    args = [recv, weight, turn, scale]
    if base is not None:
        in_specs.append(pl.BlockSpec(memory_space=pl.ANY))
        args.append(base)
    return pl.pallas_call(
        functools.partial(main_body, first, count, rows, bins, base is not None),
        grid=(MINOR,),
        in_specs=in_specs,
        out_specs=pl.BlockSpec(memory_space=pl.ANY),
        out_shape=jax.ShapeDtypeStruct((2, total, bins, PULSES), jnp.float32),
        scratch_shapes=[
            pltpu.VMEM((MINOR + 2 * PAD, 2, count, MAJOR, LANES), jnp.float32),
            pltpu.VMEM((2, 2 * MAJOR, count * LANES), jnp.float32),
            pltpu.VMEM((MINOR, 2, 2 * MAJOR, count * LANES), jnp.float32),
            pltpu.VMEM((2, 16, MAJOR, LANES), jnp.float32),
            pltpu.VMEM((2, count * rows, bins, PULSES), jnp.float32),
            pltpu.SemaphoreType.DMA((count,)),
        ],
        input_output_aliases={} if base is None else {4: 0},
        compiler_params=pltpu.CompilerParams(vmem_limit_bytes=58 * 2**20),
        cost_estimate=pl.CostEstimate(
            flops=count * 32 * 6 * 256 * 256 * 128, bytes_accessed=(36 + 4 * count) * 2**20, transcendentals=0
        ),
        name="finish",
    )(*args)


def on_device(devices, echo, spectral_shift_units):
    bins = BINS // devices
    rows = LANES // bins
    lead = echo.shape[1] * echo.shape[2]
    flat = echo.reshape((2, lead) + echo.shape[3:])
    units = lead // rows
    cuts = (0, units - 1, units) if units > 1 else (0, units)
    codes = lax.dynamic_slice_in_dim(spectral_shift_units, lax.axis_index("pulse") * bins, bins, 0)
    received = []
    for first, last in zip(cuts[:-1], cuts[1:]):
        sent = pack(flat, first, last - first, devices)
        received.append(lax.all_to_all(sent, "pulse", 0, 0, tiled=True))
    weight = weights(jnp.tile(codes, rows))
    turn = jnp.asarray(turns())
    scale = correction(PULSES).reshape(1, PULSES)
    out = None
    for first, recv in zip(cuts[:-1], received):
        out = finish(recv, weight, turn, scale, out, first, lead)
    return out.reshape(echo.shape[:3] + (bins, PULSES))


def solution(mesh):
    placed = (P(None, "grp", None, "pulse", None), P())
    return jax.shard_map(
        functools.partial(on_device, mesh.shape["pulse"]),
        mesh=mesh,
        in_specs=placed,
        out_specs=P(None, "grp", None, "pulse", None),
        check_vma=False,
    )
```

time: 1200 us -> 308 us (0.26); the launches traced: 1180 us -> 306 us
  matrix products: 573 us -> 0 us
  local copies, waits for them, and re-layouts: 394 us -> 1.42 us
  Pallas kernels: 0 us -> 137 us
  other arithmetic: 56.5 us -> 24.4 us
  waiting for transfers between devices: 148 us -> 131 us
    dot_general x16 -> x0, matrix products: 573 us -> none  [the longest x8 246 us: one_block(): jnp.einsum('zcypk,kpw->zcykw', segment, weight, precision=lax.Precision.H...]
    scatter-add x2 -> x0, local copies, waits for them, and re-layouts: 217 us -> none  [the longest x1 168 us: on_device(): middle = middle.at[..., 2 * per_device - rim_cells:].add(left_parts)]
    pallas_call x0 -> x5, Pallas kernels: none -> 137 us  [the longest x2 63.6 us: finish(): pl.pallas_call(functools.partial(main_body, first, count, rows, bins, bas...]
    slice x4 -> x0, local copies, waits for them, and re-layouts: 40.1 us -> none  [the longest x2 14.7 us: on_device(): jnp.roll(extended[..., rim_cells + 2 * per_device:], 1, axis=4)]
    reshape x2 -> x0, local copies, waits for them, and re-layouts: 29.5 us -> none  [the longest x1 14.7 us: transform(): out_imag = out_imag.reshape(lead_shape + (grid_size,))]
    another operation x2 -> x1, local copies, waits for them, and re-layouts: 25.4 us -> 0.01 us  [on_device(): weight = weights(jnp.tile(codes, rows))]
    dynamic_update_slice x8 -> x0, local copies, waits for them, and re-layouts: 21.2 us -> none  [spread(): lax.map(one_block, jnp.arange(number_of_keys // block_rows, dtype=jnp.int...]
    all_to_all x1 -> x2, waiting for transfers between devices: 148 us -> 131 us  [on_device(): received.append(lax.all_to_all(sent, 'pulse', 0, 0, tiled=True))]
  transfers between devices with their start and end apart: 1 -> 2, of which waited for: 1 -> 1; matrix products, arithmetic and copies ran while one was open for 3% -> 8% of each run, Pallas kernels for 0% -> 32%
where the time goes in v1:
time: 308 us; the launch traced here: 306 us
  Pallas kernels  137 us (44%)
  waiting for transfers between devices  131 us (43%)
  other arithmetic  24.4 us (8%)
  starting transfers between devices  11.5 us (4%)
    all_to_all x2, waiting for transfers between devices, on_device(): received.append(lax.all_to_all(sent, 'pulse', 0, 0, tiled=True))  131 us
    pallas_call x2, Pallas kernels, finish(): pl.pallas_call(functools.partial(main_body, first, count, rows, bins, bas...  63.6 us
    pallas_call x1, Pallas kernels, weights(): pl.pallas_call(weight_body, grid=(MINOR,), in_specs=[whole, whole], out_s...  51.6 us
    pallas_call x2, Pallas kernels, pack(): pl.pallas_call(functools.partial(pack_body, rows, bins), grid=(count, BIN...  22 us
    div x1, other arithmetic, weights(): (numerator - cell_floor * denominator).astype(jnp.float32)  11.5 us
    all_to_all x2, starting transfers between devices, on_device(): received.append(lax.all_to_all(sent, 'pulse', 0, 0, tiled=True))  11.5 us
    sub x1, other arithmetic, weights(): shift = cell_floor - 2 * slow  11.4 us
  transfers between devices with their start and end apart: 2, of which 1 were waited for; matrix products, arithmetic and copies ran while one was open for 8% of the time, Pallas kernels for 32%

profile of v1, /device:TPU:15, one launch (start us, length us, event | category | flops | bytes accessed | tf_op | source)
XLA Modules:
  0.0 305.8 jit_solution(8461429231630831783)
XLA Ops:
  0.0 15.9 %pack.3 = f32[16,3,2,128,128]{4,3,2,1,0:T(8,128)} custom-call(f32[2,8,128,1024]{3,2,1,0:T(8,128)} %bitcast.2), custom_call_target="tpu_custom_call" | custom-call | bytes 12582912 | tf_op jit(solution)/shard_map/pack/pallas_call | solution.py:112
  15.9 6.6 %all-to-all-start.1 = ((f32[16,3,2,128,128]{4,3,2,1,0:T(8,128)}), f32[16,3,2,128,128]{4,3,2,1,0:T(8,128)}, u32[]{:S(2)}, u32[]{:S(2)}) async-start(f32[16,3,2,128,128]{4,3,2,1,0:T(8,128)} %pack.3), calls=%async_computation.1 | async-start | bytes 12582912 | tf_op jit(solution)/shard_map/all_to_all | solution.py:406
  22.5 6.1 %pack.2 = f32[16,1,2,128,128]{4,3,2,1,0:T(8,128)} custom-call(f32[2,8,128,1024]{3,2,1,0:T(8,128)} %bitcast.3), custom_call_target="tpu_custom_call" | custom-call | bytes 4194304 | tf_op jit(solution)/shard_map/pack/pallas_call | solution.py:112
  28.6 131.3 %all-to-all-done.1.recv_ref = f32[16,3,2,128,128]{4,3,2,1,0:T(8,128)} async-done(((f32[16,3,2,128,128]{4,3,2,1,0:T(8,128)}), f32[16,3,2,128,128]{4,3,2,1,0:T(8,128)}, u32[]{:S(2)}, u32[]{:S(2)}) %all-to-all-start.1) | async-done | bytes 6291488 | tf_op jit(solution)/shard_map/all_to_all | solution.py:406
  159.9 4.9 %all-to-all-start = ((f32[16,1,2,128,128]{4,3,2,1,0:T(8,128)}), f32[16,1,2,128,128]{4,3,2,1,0:T(8,128)S(1)}, u32[]{:S(2)}, u32[]{:S(2)}) async-start(f32[16,1,2,128,128]{4,3,2,1,0:T(8,128)} %pack.2), calls=%async_computation | async-start | bytes 4194304 | tf_op jit(solution)/shard_map/all_to_all | solution.py:406
  164.8 0.8 dynamic-slice_add_fusion
  165.6 0.1 add.112
  165.7 11.4 %fusion.1.shift_ref = s32[16,128,128]{2,1,0:T(8,128)} fusion(s32[16,128]{1,0:T(8,128)S(1)} %get-tuple-element.8, s32[128]{0:T(128)S(1)} %add.112, s32[16,128]{1,0:T(8,128)S(1)} %get-tuple-element.9, s32[128]{0:T(128)S(1)} %get-tuple-element.6, s32[16,128]{1,0:T(8,128)S(1)} %get-tuple-element.7), kind=kLoop, calls=%fused_computation.4 | loop fusion | flops 2097152 | bytes 1074176 | tf_op jit(solution)/shard_map/sub | solution.py:191
  177.1 11.5 %convert_divide_fusion.fraction_ref = f32[16,128,128]{2,1,0:T(8,128)} fusion(f32[128]{0:T(128)S(1)} %get-tuple-element.5, s32[128]{0:T(128)S(1)} %add.112, s32[16,128]{1,0:T(8,128)S(1)} %get-tuple-element.9, s32[128]{0:T(128)S(1)} %get-tuple-element.6, s32[16,128]{1,0:T(8,128)S(1)} %get-tuple-element.7), kind=kLoop, calls=%fused_computation.1 | loop fusion | flops 2883584 | bytes 1066496 | tf_op jit(solution)/shard_map/div | solution.py:190
  188.6 51.6 %weights.1.weight_ref = f32[16,416,8,128]{3,2,1,0:T(8,128)} custom-call(s32[16,128,128]{2,1,0:T(8,128)} %fusion.1.shift_ref, f32[16,128,128]{2,1,0:T(8,128)} %convert_divide_fusion.fraction_ref), custom_call_target="tpu_custom_call" | custom-call | flops 838860800 | bytes 67108864 | tf_op jit(solution)/shard_map/weights/pallas_call | solution.py:194
  240.1 0.7 fusion.10.scale_ref
  240.9 39.0 %finish.2.rest_0_ = f32[2,8,64,2048]{3,2,1,0:T(8,128)} custom-call(f32[16,3,2,128,128]{4,3,2,1,0:T(8,128)} %all-to-all-done.1.recv_ref, f32[16,416,8,128]{3,2,1,0:T(8,128)} %weights.1.weight_ref, bf16[16,2,2,256,256]{4,3,2,1,0:T(8,128)(2,1)} %constant.64.clone.turn_ref, f32[1,2048]{1,0:T(1,128)} %fusion.10.scale_ref), custom_call_target="tpu_custom_call" | custom-call | flops 4831838208 | bytes 50331648 | tf_op jit(solution)/shard_map/finish/pallas_call | solution.py:372
  279.8 0.0 all-to-all-done.recv_ref
  279.9 0.0 copy-start
  279.9 1.3 copy-done
  281.2 24.6 %finish.3 = f32[2,8,64,2048]{3,2,1,0:T(8,128)} custom-call(f32[16,1,2,128,128]{4,3,2,1,0:T(8,128)} %copy-done, f32[16,416,8,128]{3,2,1,0:T(8,128)} %weights.1.weight_ref, bf16[16,2,2,256,256]{4,3,2,1,0:T(8,128)(2,1)} %constant.64.clone.turn_ref, f32[1,2048]{1,0:T(1,128)} %fusion.10.scale_ref, ...), custom_call_target="tpu_custom_call", output_to_operand_aliasing={{}: (4, {})} | custom-call | flops 1610612736 | bytes 41943040 | tf_op jit(solution)/shard_map/finish/pallas_call | solution.py:372
  (4 shorter events, 0.0 us)
Async XLA Ops:
  15.9 144.0 %all-to-all-start.1 = ((f32[16,3,2,128,128]{4,3,2,1,0:T(8,128)}), f32[16,3,2,128,128]{4,3,2,1,0:T(8,128)}, u32[]{:S(2)}, u32[]{:S(2)}) async-start(f32[16,3,2,128,128]{4,3,2,1,0:T(8,128)} %pack.3), calls=%async_computation.1 | async-start | bytes 12582912 | tf_op jit(solution)/shard_map/all_to_all | solution.py:406
  159.9 120.0 %all-to-all-start = ((f32[16,1,2,128,128]{4,3,2,1,0:T(8,128)}), f32[16,1,2,128,128]{4,3,2,1,0:T(8,128)S(1)}, u32[]{:S(2)}, u32[]{:S(2)}) async-start(f32[16,1,2,128,128]{4,3,2,1,0:T(8,128)} %pack.2), calls=%async_computation | async-start | bytes 4194304 | tf_op jit(solution)/shard_map/all_to_all | solution.py:406
  279.9 1.3 copy-start

commit v2 on v1

--- a/solution.py
+++ b/solution.py
@@ -50,18 +50,14 @@
     low, high = ends.min(0) - 3, ends.max(0) + 4
     out, start = [], 0
     for block in range(BLOCKS):
-        row = []
         pairs = np.arange(128 * block, 128 * (block + 1))
-        for parity in range(2):
-            offsets = []
-            for e in range(-PAD, PAD + 1):
-                source = (pairs - e) % PULSES
-                reach = 2 * e + parity
-                if np.any((low[source] <= reach) & (reach <= high[source])):
-                    offsets.append(e)
-            row.append((start, tuple(offsets)))
-            start += len(offsets)
-        out.append(tuple(row))
+        offsets = []
+        for e in range(-PAD, PAD + 1):
+            source = (pairs - e) % PULSES
+            if np.any((low[source] <= 2 * e + 1) & (2 * e <= high[source])):
+                offsets.append(e)
+        out.append((start, tuple(offsets)))
+        start += len(offsets)
     return tuple(out), start
 
 
@@ -131,8 +127,9 @@
         store(m1 + MINOR + PAD, pltpu.roll(ref(m1 + PAD), MAJOR - 1, 0))
 
 
-def weight_body(shift_ref, fraction_ref, out_ref, taps, shifts):
+def weight_body(bins, shift_ref, fraction_ref, out_ref, taps, shifts):
     q1 = pl.program_id(0)
+    parity = lax.broadcasted_iota(jnp.int32, (MAJOR, LANES), 1) // bins % 2
 
     @pl.when(q1 == 0)
     def _():
@@ -140,7 +137,7 @@
 
         @pl.loop(0, MINOR)
         def _(m1):
-            shifts[PAD + m1] = shift_ref[m1]
+            shifts[PAD + m1] = shift_ref[m1] - parity
 
             @pl.loop(0, BLOCKS)
             def _(block):
@@ -169,18 +166,17 @@
     table, _ = windows()
     for block in range(BLOCKS):
         at = pl.ds(8 * block, 8)
-        for parity in range(2):
-            start, offsets = table[block][parity]
-            for index, e in enumerate(offsets):
-                row = q1 - e + PAD
-                shift = shifts[row, at, :]
-                value = jnp.zeros((8, LANES), jnp.float32)
-                for tap in range(8):
-                    value = jnp.where(shift == 2 * e + parity + 3 - tap, taps[tap, row, at, :], value)
-                out_ref[0, start + index] = value
-
-
-def weights(codes):
+        start, offsets = table[block]
+        for index, e in enumerate(offsets):
+            row = q1 - e + PAD
+            shift = shifts[row, at, :]
+            value = jnp.zeros((8, LANES), jnp.float32)
+            for tap in range(8):
+                value = jnp.where(shift == 2 * e + 3 - tap, taps[tap, row, at, :], value)
+            out_ref[0, start + index] = value
+
+
+def weights(codes, bins):
     _, entries = windows()
     pulse = jnp.arange(MINOR, dtype=jnp.int32)[:, None] + MINOR * jnp.arange(MAJOR, dtype=jnp.int32)[None, :]
     slow = (pulse - PULSES // 2)[:, :, None]
@@ -192,7 +188,7 @@
     whole = pl.BlockSpec((MINOR, MAJOR, LANES), lambda q: (0, 0, 0))
     spread = MINOR + 2 * PAD
     return pl.pallas_call(
-        weight_body,
+        functools.partial(weight_body, bins),
         grid=(MINOR,),
         in_specs=[whole, whole],
         out_specs=pl.BlockSpec((1, entries, 8, LANES), lambda q: (q, 0, 0, 0)),
@@ -286,21 +282,25 @@
                 extend(lambda row: spread[row, part, unit], keep)
 
     table, _ = windows()
-    for parity in range(2):
-        for block in range(BLOCKS):
-            start, offsets = table[block][parity]
-            sums = [[None] * count, [None] * count]
-            for index, e in enumerate(offsets):
-                weight = weight_ref[0, start + index]
-                row = q1 - e + PAD
-                for part in range(2):
-                    for unit in range(count):
-                        term = weight * spread[row, part, unit, pl.ds(8 * block, 8), :]
-                        held = sums[part][unit]
-                        sums[part][unit] = term if held is None else held + term
+    first_parity = lax.broadcasted_iota(jnp.int32, (8, LANES), 1) // bins % 2 == 0
+    for block in range(BLOCKS):
+        start, offsets = table[block]
+        sums = {}
+        for index, e in enumerate(offsets):
+            both = weight_ref[0, start + index]
+            ahead = pltpu.roll(both, bins, 1)
+            behind = ahead if 2 * bins == LANES else pltpu.roll(both, LANES - bins, 1)
+            weight = (jnp.where(first_parity, both, ahead), jnp.where(first_parity, behind, both))
+            row = q1 - e + PAD
             for part in range(2):
                 for unit in range(count):
-                    pairs[parity, pl.ds(part * MAJOR + 8 * block, 8), pl.ds(unit * LANES, LANES)] = sums[part][unit]
+                    sample = spread[row, part, unit, pl.ds(8 * block, 8), :]
+                    for parity in range(2):
+                        term = weight[parity] * sample
+                        key = (parity, part, unit)
+                        sums[key] = sums[key] + term if key in sums else term
+        for (parity, part, unit), value in sums.items():
+            pairs[parity, pl.ds(part * MAJOR + 8 * block, 8), pl.ds(unit * LANES, LANES)] = value
     for parity in range(2):
         full = pairs[parity]
         high = full.astype(jnp.bfloat16)
@@ -400,11 +400,12 @@
     units = lead // rows
     cuts = (0, units - 1, units) if units > 1 else (0, units)
     codes = lax.dynamic_slice_in_dim(spectral_shift_units, lax.axis_index("pulse") * bins, bins, 0)
-    received = []
-    for first, last in zip(cuts[:-1], cuts[1:]):
-        sent = pack(flat, first, last - first, devices)
-        received.append(lax.all_to_all(sent, "pulse", 0, 0, tiled=True))
-    weight = weights(jnp.tile(codes, rows))
+    sent = [pack(flat, first, last - first, devices) for first, last in zip(cuts[:-1], cuts[1:])]
+    weight = weights(jnp.tile(codes, rows), bins)
+    received = [lax.all_to_all(sent[0], "pulse", 0, 0, tiled=True)]
+    for later in sent[1:]:
+        later, weight = lax.optimization_barrier((later, weight))
+        received.append(lax.all_to_all(later, "pulse", 0, 0, tiled=True))
     turn = jnp.asarray(turns())
     scale = correction(PULSES).reshape(1, PULSES)
     out = None

time: 308 us -> 238 us (0.77)
  waiting for transfers between devices: 131 us -> 72.7 us
  Pallas kernels: 137 us -> 127 us
    all_to_all x2, waiting for transfers between devices: 131 us -> 72.7 us  [the longest x1 65.8 us: on_device(): received = [lax.all_to_all(sent[0], 'pulse', 0, 0, tiled=True)]]
    pallas_call x1, Pallas kernels: 51.6 us -> 41.7 us  [weights(): pl.pallas_call(functools.partial(weight_body, bins), grid=(MINOR,), in_sp...]
  transfers between devices with their start and end apart: 2 -> 2, of which waited for: 1 -> 2; matrix products, arithmetic and copies ran while one was open for 8% -> 10% of each run, Pallas kernels for 32% -> 37%
where the time goes in v2:
time: 238 us; the launch traced here: 237 us
  Pallas kernels  127 us (53%)
  waiting for transfers between devices  72.7 us (31%)
  other arithmetic  24.4 us (10%)
  starting transfers between devices  11.5 us (5%)
    all_to_all x1, waiting for transfers between devices, on_device(): received = [lax.all_to_all(sent[0], 'pulse', 0, 0, tiled=True)]  65.8 us
    pallas_call x2, Pallas kernels, finish(): pl.pallas_call(functools.partial(main_body, first, count, rows, bins, bas...  63.1 us
    pallas_call x1, Pallas kernels, weights(): pl.pallas_call(functools.partial(weight_body, bins), grid=(MINOR,), in_sp...  41.7 us
    pallas_call x2, Pallas kernels, pack(): pl.pallas_call(functools.partial(pack_body, rows, bins), grid=(count, BIN...  22.1 us
    div x1, other arithmetic, weights(): (numerator - cell_floor * denominator).astype(jnp.float32)  11.5 us
    sub x1, other arithmetic, weights(): shift = cell_floor - 2 * slow  11.4 us
    all_to_all x1, waiting for transfers between devices, on_device(): received.append(lax.all_to_all(later, 'pulse', 0, 0, tiled=True))  6.89 us
    all_to_all x1, starting transfers between devices, on_device(): received = [lax.all_to_all(sent[0], 'pulse', 0, 0, tiled=True)]  6.55 us
  transfers between devices with their start and end apart: 2, of which 2 were waited for; matrix products, arithmetic and copies ran while one was open for 10% of the time, Pallas kernels for 37%

profile of v2, /device:TPU:15, one launch (start us, length us, event | category | flops | bytes accessed | tf_op | source)
XLA Modules:
  0.0 236.8 jit_solution(1190549692786601110)
XLA Ops:
  0.0 15.9 %pack.3 = f32[16,3,2,128,128]{4,3,2,1,0:T(8,128)} custom-call(f32[2,8,128,1024]{3,2,1,0:T(8,128)} %bitcast.2), custom_call_target="tpu_custom_call" | custom-call | bytes 12582912 | tf_op jit(solution)/shard_map/pack/pallas_call | solution.py:108
  15.9 6.6 %all-to-all-start.1 = ((f32[16,3,2,128,128]{4,3,2,1,0:T(8,128)}), f32[16,3,2,128,128]{4,3,2,1,0:T(8,128)}, u32[]{:S(2)}, u32[]{:S(2)}) async-start(f32[16,3,2,128,128]{4,3,2,1,0:T(8,128)} %pack.3), calls=%async_computation.1 | async-start | bytes 12582912 | tf_op jit(solution)/shard_map/all_to_all | solution.py:405
  22.5 6.1 %pack.2 = f32[16,1,2,128,128]{4,3,2,1,0:T(8,128)} custom-call(f32[2,8,128,1024]{3,2,1,0:T(8,128)} %bitcast.3), custom_call_target="tpu_custom_call" | custom-call | bytes 4194304 | tf_op jit(solution)/shard_map/pack/pallas_call | solution.py:108
  28.6 0.8 dynamic-slice_add_fusion
  29.4 0.1 add.112
  29.5 11.4 %fusion.1.shift_ref = s32[16,128,128]{2,1,0:T(8,128)} fusion(s32[16,128]{1,0:T(8,128)S(1)} %get-tuple-element.12, s32[128]{0:T(128)S(1)} %add.112, s32[16,128]{1,0:T(8,128)S(1)} %get-tuple-element.13, s32[128]{0:T(128)S(1)} %get-tuple-element.10, s32[16,128]{1,0:T(8,128)S(1)} %get-tuple-element.11), kind=kLoop, calls=%fused_computation.4 | loop fusion | flops 2097152 | bytes 1074176 | tf_op jit(solution)/shard_map/sub | solution.py:187
  40.9 11.5 %convert_divide_fusion.fraction_ref = f32[16,128,128]{2,1,0:T(8,128)} fusion(f32[128]{0:T(128)S(1)} %get-tuple-element.9, s32[128]{0:T(128)S(1)} %add.112, s32[16,128]{1,0:T(8,128)S(1)} %get-tuple-element.13, s32[128]{0:T(128)S(1)} %get-tuple-element.10, s32[16,128]{1,0:T(8,128)S(1)} %get-tuple-element.11), kind=kLoop, calls=%fused_computation.1 | loop fusion | flops 2883584 | bytes 1066496 | tf_op jit(solution)/shard_map/div | solution.py:186
  52.4 41.7 %weights.1.weight_ref = f32[16,216,8,128]{3,2,1,0:T(8,128)} custom-call(s32[16,128,128]{2,1,0:T(8,128)} %fusion.1.shift_ref, f32[16,128,128]{2,1,0:T(8,128)} %convert_divide_fusion.fraction_ref), custom_call_target="tpu_custom_call" | custom-call | flops 838860800 | bytes 67108864 | tf_op jit(solution)/shard_map/weights/pallas_call | solution.py:190
  94.1 65.8 %all-to-all-done.1.recv_ref = f32[16,3,2,128,128]{4,3,2,1,0:T(8,128)} async-done(((f32[16,3,2,128,128]{4,3,2,1,0:T(8,128)}), f32[16,3,2,128,128]{4,3,2,1,0:T(8,128)}, u32[]{:S(2)}, u32[]{:S(2)}) %all-to-all-start.1) | async-done | bytes 6291488 | tf_op jit(solution)/shard_map/all_to_all | solution.py:405
  159.9 4.9 %all-to-all-start = ((f32[16,1,2,128,128]{4,3,2,1,0:T(8,128)}), f32[16,1,2,128,128]{4,3,2,1,0:T(8,128)S(1)}, u32[]{:S(2)}, u32[]{:S(2)}) async-start(f32[16,1,2,128,128]{4,3,2,1,0:T(8,128)} %pack.2), calls=%async_computation | async-start | bytes 4194304 | tf_op jit(solution)/shard_map/all_to_all | solution.py:408
  164.8 0.7 fusion.10.scale_ref
  165.5 39.8 %finish.2.rest_0_ = f32[2,8,64,2048]{3,2,1,0:T(8,128)} custom-call(f32[16,3,2,128,128]{4,3,2,1,0:T(8,128)} %all-to-all-done.1.recv_ref, f32[16,216,8,128]{3,2,1,0:T(8,128)} %weights.1.weight_ref, bf16[16,2,2,256,256]{4,3,2,1,0:T(8,128)(2,1)} %constant.64.clone.turn_ref, f32[1,2048]{1,0:T(1,128)} %fusion.10.scale_ref), custom_call_target="tpu_custom_call" | custom-call | flops 4831838208 | bytes 50331648 | tf_op jit(solution)/shard_map/finish/pallas_call | solution.py:372
  205.3 6.9 %all-to-all-done.recv_ref = f32[16,1,2,128,128]{4,3,2,1,0:T(8,128)S(1)} async-done(((f32[16,1,2,128,128]{4,3,2,1,0:T(8,128)}), f32[16,1,2,128,128]{4,3,2,1,0:T(8,128)S(1)}, u32[]{:S(2)}, u32[]{:S(2)}) %all-to-all-start) | async-done | bytes 2097184 | tf_op jit(solution)/shard_map/all_to_all | solution.py:408
  212.2 0.0 copy-start
  212.2 1.3 copy-done
  213.5 23.3 %finish.3 = f32[2,8,64,2048]{3,2,1,0:T(8,128)} custom-call(f32[16,1,2,128,128]{4,3,2,1,0:T(8,128)} %copy-done, f32[16,216,8,128]{3,2,1,0:T(8,128)} %weights.1.weight_ref, bf16[16,2,2,256,256]{4,3,2,1,0:T(8,128)(2,1)} %constant.64.clone.turn_ref, f32[1,2048]{1,0:T(1,128)} %fusion.10.scale_ref, ...), custom_call_target="tpu_custom_call", output_to_operand_aliasing={{}: (4, {})} | custom-call | flops 1610612736 | bytes 41943040 | tf_op jit(solution)/shard_map/finish/pallas_call | solution.py:372
  (4 shorter events, 0.0 us)
Async XLA Ops:
  15.9 144.0 %all-to-all-start.1 = ((f32[16,3,2,128,128]{4,3,2,1,0:T(8,128)}), f32[16,3,2,128,128]{4,3,2,1,0:T(8,128)}, u32[]{:S(2)}, u32[]{:S(2)}) async-start(f32[16,3,2,128,128]{4,3,2,1,0:T(8,128)} %pack.3), calls=%async_computation.1 | async-start | bytes 12582912 | tf_op jit(solution)/shard_map/all_to_all | solution.py:405
  159.9 52.3 %all-to-all-start = ((f32[16,1,2,128,128]{4,3,2,1,0:T(8,128)}), f32[16,1,2,128,128]{4,3,2,1,0:T(8,128)S(1)}, u32[]{:S(2)}, u32[]{:S(2)}) async-start(f32[16,1,2,128,128]{4,3,2,1,0:T(8,128)} %pack.2), calls=%async_computation | async-start | bytes 4194304 | tf_op jit(solution)/shard_map/all_to_all | solution.py:408
  212.2 1.3 copy-start

commit v3 on v2

--- a/solution.py
+++ b/solution.py
@@ -87,18 +87,22 @@
 
 
 def pack_body(rows, bins, echo_ref, out_ref):
-    depth = echo_ref.shape[2] // MINOR
-    lane = lax.broadcasted_iota(jnp.int32, (depth, LANES), 1) // bins
-    for part in range(2):
-        for m1 in range(MINOR):
-            taken = [echo_ref[part, row, pl.ds(m1, depth, stride=MINOR), :] for row in range(rows)]
+    held = echo_ref.shape[2]
+    depth = held // MINOR
+    lane = lax.broadcasted_iota(jnp.int32, (8, LANES), 1) // bins
+    for column in range(BINS // LANES):
+        for group in range(held // 8):
+            taken = [
+                echo_ref[0, row, pl.ds(8 * group, 8), pl.ds(column * LANES, LANES)] for row in range(rows)
+            ]
+            to = pl.ds(8 * group % MINOR * depth + 8 * group // MINOR, 8, stride=depth)
             for dest in range(rows):
                 value = None
                 for row in range(rows):
                     turn = (row - dest) * bins % LANES
                     moved = pltpu.roll(taken[row], turn, 1) if turn else taken[row]
                     value = moved if value is None else jnp.where(lane == row, moved, value)
-                out_ref[dest, 0, part, pl.ds(m1 * depth, depth), :] = value
+                out_ref[column * rows + dest, 0, 0, to, :] = value
 
 
 def pack(echo, first, count, devices):
@@ -107,12 +111,13 @@
     held = echo.shape[2]
     return pl.pallas_call(
         functools.partial(pack_body, rows, bins),
-        grid=(count, BINS // LANES),
+        grid=(count, 2),
         in_specs=[
-            pl.BlockSpec((2, rows, held, LANES), lambda u, c: (0, u + first, 0, c)),
+            pl.BlockSpec((1, rows, held, BINS), lambda u, part: (part, u + first, 0, 0)),
         ],
-        out_specs=pl.BlockSpec((rows, 1, 2, held, LANES), lambda u, c: (c, u, 0, 0, 0)),
+        out_specs=pl.BlockSpec((devices, 1, 1, held, LANES), lambda u, part: (0, u, part, 0, 0)),
         out_shape=jax.ShapeDtypeStruct((devices, count, 2, held, LANES), jnp.float32),
+        compiler_params=pltpu.CompilerParams(vmem_limit_bytes=56 * 2**20),
         cost_estimate=pl.CostEstimate(
             flops=0, bytes_accessed=16 * devices * count * held * LANES, transcendentals=0
         ),
@@ -259,11 +264,28 @@
     return result
 
 
-def main_body(first, count, rows, bins, has_base, recv_ref, weight_ref, turn_ref, scale_ref, *rest):
+def main_body(first, count, rows, bins, has_base, close, recv_ref, weight_ref, turn_ref, scale_ref, *rest):
     if has_base:
         rest = rest[1:]
-    out_ref, spread, pairs, mids, tall, wide, sem = rest
+    out_ref, spread, pairs, mids, tall, wide, sem = rest[:7]
     q1 = pl.program_id(0)
+    before = jnp.maximum(q1 - 1, 0)
+    if close:
+        weight_far, turn_far = weight_ref, turn_ref
+        weight_ref, turn_ref, fetched = rest[7:]
+
+        def fetch_weight(q):
+            return pltpu.make_async_copy(weight_far.at[q], weight_ref.at[q], fetched.at[0, q])
+
+        def fetch_turn(q):
+            return pltpu.make_async_copy(turn_far.at[q], turn_ref.at[q], fetched.at[1, q])
+
+        @pl.when(q1 == 0)
+        def _():
+            for q in range(MINOR):
+                fetch_weight(q).start()
+                fetch_turn(q).start()
+
     devices, depth = recv_ref.shape[0], recv_ref.shape[3] // MINOR
 
     @pl.when(q1 == 0)
@@ -281,36 +303,65 @@
 
                 extend(lambda row: spread[row, part, unit], keep)
 
-    table, _ = windows()
-    first_parity = lax.broadcasted_iota(jnp.int32, (8, LANES), 1) // bins % 2 == 0
-    for block in range(BLOCKS):
-        start, offsets = table[block]
-        sums = {}
-        for index, e in enumerate(offsets):
-            both = weight_ref[0, start + index]
-            ahead = pltpu.roll(both, bins, 1)
-            behind = ahead if 2 * bins == LANES else pltpu.roll(both, LANES - bins, 1)
-            weight = (jnp.where(first_parity, both, ahead), jnp.where(first_parity, behind, both))
-            row = q1 - e + PAD
-            for part in range(2):
-                for unit in range(count):
-                    sample = spread[row, part, unit, pl.ds(8 * block, 8), :]
-                    for parity in range(2):
-                        term = weight[parity] * sample
-                        key = (parity, part, unit)
-                        sums[key] = sums[key] + term if key in sums else term
-        for (parity, part, unit), value in sums.items():
-            pairs[parity, pl.ds(part * MAJOR + 8 * block, 8), pl.ds(unit * LANES, LANES)] = value
-    for parity in range(2):
-        full = pairs[parity]
-        high = full.astype(jnp.bfloat16)
-        low = (full - high.astype(jnp.float32)).astype(jnp.bfloat16)
-        turn_high, turn_low = turn_ref[0, parity, 0], turn_ref[0, parity, 1]
+    def combine():
+        turn_at = before if close else 0
         dot = functools.partial(jnp.dot, preferred_element_type=jnp.float32)
-        mids[q1, parity] = dot(turn_high, high) + (dot(turn_high, low) + dot(turn_low, high))
-
-    @pl.when(q1 == MINOR - 1)
+        width = count * LANES
+        for parity in range(2):
+            full = pairs[parity]
+            high = full.astype(jnp.bfloat16)
+            low = (full - high.astype(jnp.float32)).astype(jnp.bfloat16)
+            turn_high, turn_low = turn_ref[turn_at, parity, 0], turn_ref[turn_at, parity, 1]
+            if count == 1:
+                both = dot(turn_high, jnp.concatenate([high, low], 1))
+                mids[before, parity] = both[:, :width] + (both[:, width:] + dot(turn_low, high))
+            else:
+                mids[before, parity] = dot(turn_high, high) + (dot(turn_high, low) + dot(turn_low, high))
+
+    if close:
+        @pl.when(q1 < MINOR)
+        def _():
+            fetch_weight(q1).wait()
+
+        @pl.when(q1 != 1)
+        def _():
+            fetch_turn(before).wait()
+
+    @pl.when(q1 < MINOR)
     def _():
+        combine()
+        weight_at = q1 if close else 0
+        table, _ = windows()
+        first_parity = lax.broadcasted_iota(jnp.int32, (8, LANES), 1) // bins % 2 == 0
+        for block in range(BLOCKS):
+            start, offsets = table[block]
+            sums = {}
+            for index, e in enumerate(offsets):
+                both = weight_ref[weight_at, start + index]
+                ahead = pltpu.roll(both, bins, 1)
+                behind = ahead if 2 * bins == LANES else pltpu.roll(both, LANES - bins, 1)
+                weight = (jnp.where(first_parity, both, ahead), jnp.where(first_parity, behind, both))
+                row = q1 - e + PAD
+                for part in range(2):
+                    for unit in range(count):
+                        sample = spread[row, part, unit, pl.ds(8 * block, 8), :]
+                        for parity in range(2):
+                            term = weight[parity] * sample
+                            key = (parity, part, unit)
+                            sums[key] = sums[key] + term if key in sums else term
+            for (parity, part, unit), value in sums.items():
+                pairs[parity, pl.ds(part * MAJOR + 8 * block, 8), pl.ds(unit * LANES, LANES)] = value
+
+    def leave(unit, part):
+        return pltpu.make_async_copy(
+            wide.at[part],
+            out_ref.at[part, pl.ds((first + unit) * rows, rows)],
+            sem.at[unit, part],
+        )
+
+    @pl.when(q1 == MINOR)
+    def _():
+        combine()
         for unit in range(count):
             across = pl.ds(unit * LANES, LANES)
 
@@ -330,27 +381,22 @@
                     for part in range(2):
                         tall[part, n1, pl.ds(pl.multiple_of(8 * block, 8), 8), :] = value[part]
 
-            @pl.loop(0, 16)
-            def _(n1):
-                at = pl.ds(pl.multiple_of(n1 * LANES, LANES), LANES)
-                scale = scale_ref[pl.ds(0, 1), at]
-                for part in range(2):
-                    turned = jnp.transpose(tall[part, n1]) * scale
-                    for row in range(rows):
-                        wide[part, unit * rows + row, :, at] = turned[row * bins : (row + 1) * bins]
-
-            copy = pltpu.make_async_copy(
-                wide.at[:, pl.ds(unit * rows, rows)],
-                out_ref.at[:, pl.ds((first + unit) * rows, rows)],
-                sem.at[unit],
-            )
-            copy.start()
-        for unit in range(count):
-            pltpu.make_async_copy(
-                wide.at[:, pl.ds(unit * rows, rows)],
-                out_ref.at[:, pl.ds((first + unit) * rows, rows)],
-                sem.at[unit],
-            ).wait()
+            for part in range(2):
+                if unit:
+                    leave(unit - 1, part).wait()
+
+                @pl.loop(0, 4)
+                def _(group):
+                    for member in range(4):
+                        n1 = 4 * group + member
+                        at = pl.ds(pl.multiple_of(n1 * LANES, LANES), LANES)
+                        turned = jnp.transpose(tall[part, n1]) * scale_ref[pl.ds(0, 1), at]
+                        for row in range(rows):
+                            wide[part, row, :, at] = turned[row * bins : (row + 1) * bins]
+
+                leave(unit, part).start()
+        for part in range(2):
+            leave(count - 1, part).wait()
 
 
 def finish(recv, weight, turn, scale, base, first, total):
@@ -358,20 +404,34 @@
     bins = BINS // devices
     rows = LANES // bins
     _, entries = windows()
-    one = pl.Buffered(1)
-    in_specs = [
-        pl.BlockSpec(recv.shape, lambda q: (0, 0, 0, 0, 0), pipeline_mode=one),
-        pl.BlockSpec((1, entries, 8, LANES), lambda q: (q, 0, 0, 0)),
-        pl.BlockSpec((1, 2, 2, 2 * MAJOR, 2 * MAJOR), lambda q: (q, 0, 0, 0, 0)),
-        pl.BlockSpec((1, PULSES), lambda q: (0, 0)),
-    ]
+    close = count == 1
+    if close:
+        in_specs = [
+            pl.BlockSpec(memory_space=pltpu.VMEM),
+            pl.BlockSpec(memory_space=pl.ANY),
+            pl.BlockSpec(memory_space=pl.ANY),
+        ]
+    else:
+        in_specs = [
+            pl.BlockSpec(recv.shape, lambda q: (0, 0, 0, 0, 0), pipeline_mode=pl.Buffered(1)),
+            pl.BlockSpec((1, entries, 8, LANES), lambda q: (jnp.minimum(q, MINOR - 1), 0, 0, 0)),
+            pl.BlockSpec((1, 2, 2, 2 * MAJOR, 2 * MAJOR), lambda q: (jnp.maximum(q - 1, 0), 0, 0, 0, 0)),
+        ]
+    in_specs.append(pl.BlockSpec((1, PULSES), lambda q: (0, 0)))
     args = [recv, weight, turn, scale]
     if base is not None:
         in_specs.append(pl.BlockSpec(memory_space=pl.ANY))
         args.append(base)
+    ahead = []
+    if close:
+        ahead = [
+            pltpu.VMEM(weight.shape, jnp.float32),
+            pltpu.VMEM(turn.shape, jnp.bfloat16),
+            pltpu.SemaphoreType.DMA((2, MINOR)),
+        ]
     return pl.pallas_call(
-        functools.partial(main_body, first, count, rows, bins, base is not None),
-        grid=(MINOR,),
+        functools.partial(main_body, first, count, rows, bins, base is not None, close),
+        grid=(MINOR + 1,),
         in_specs=in_specs,
         out_specs=pl.BlockSpec(memory_space=pl.ANY),
         out_shape=jax.ShapeDtypeStruct((2, total, bins, PULSES), jnp.float32),
@@ -380,11 +440,12 @@
             pltpu.VMEM((2, 2 * MAJOR, count * LANES), jnp.float32),
             pltpu.VMEM((MINOR, 2, 2 * MAJOR, count * LANES), jnp.float32),
             pltpu.VMEM((2, 16, MAJOR, LANES), jnp.float32),
-            pltpu.VMEM((2, count * rows, bins, PULSES), jnp.float32),
-            pltpu.SemaphoreType.DMA((count,)),
-        ],
+            pltpu.VMEM((2, rows, bins, PULSES), jnp.float32),
+            pltpu.SemaphoreType.DMA((count, 2)),
+        ]
+        + ahead,
         input_output_aliases={} if base is None else {4: 0},
-        compiler_params=pltpu.CompilerParams(vmem_limit_bytes=58 * 2**20),
+        compiler_params=pltpu.CompilerParams(vmem_limit_bytes=(54 if close else 58) * 2**20),
         cost_estimate=pl.CostEstimate(
             flops=count * 32 * 6 * 256 * 256 * 128, bytes_accessed=(36 + 4 * count) * 2**20, transcendentals=0
         ),

time: 238 us -> 220 us (0.924)
  Pallas kernels: 127 us -> 99.8 us
  waiting for transfers between devices: 72.7 us -> 82.1 us
    pallas_call x2, Pallas kernels: 63.1 us -> 47.5 us  [finish(): pl.pallas_call(functools.partial(main_body, first, count, rows, bins, bas...]
    pallas_call x2, Pallas kernels: 22.1 us -> 10.6 us  [pack(): pl.pallas_call(functools.partial(pack_body, rows, bins), grid=(count, 2),...]
    all_to_all x1, waiting for transfers between devices: 6.89 us -> 13.1 us  [on_device(): received.append(lax.all_to_all(later, 'pulse', 0, 0, tiled=True))]
    all_to_all x1, waiting for transfers between devices: 65.8 us -> 69 us  [on_device(): received = [lax.all_to_all(sent[0], 'pulse', 0, 0, tiled=True)]]
  transfers between devices with their start and end apart: 2 -> 2, of which waited for: 2 -> 2; matrix products, arithmetic and copies ran while one was open for 10% -> 11% of each run, Pallas kernels for 37% -> 36%
where the time goes in v3:
time: 220 us; the launch traced here: 219 us
  Pallas kernels  99.8 us (45%)
  waiting for transfers between devices  82.1 us (37%)
  other arithmetic  24.4 us (11%)
  starting transfers between devices  11.5 us (5%)
    all_to_all x1, waiting for transfers between devices, on_device(): received = [lax.all_to_all(sent[0], 'pulse', 0, 0, tiled=True)]  69 us
    pallas_call x2, Pallas kernels, finish(): pl.pallas_call(functools.partial(main_body, first, count, rows, bins, bas...  47.5 us
    pallas_call x1, Pallas kernels, weights(): pl.pallas_call(functools.partial(weight_body, bins), grid=(MINOR,), in_sp...  41.7 us
    all_to_all x1, waiting for transfers between devices, on_device(): received.append(lax.all_to_all(later, 'pulse', 0, 0, tiled=True))  13.1 us
    div x1, other arithmetic, weights(): (numerator - cell_floor * denominator).astype(jnp.float32)  11.5 us
    sub x1, other arithmetic, weights(): shift = cell_floor - 2 * slow  11.4 us
    pallas_call x2, Pallas kernels, pack(): pl.pallas_call(functools.partial(pack_body, rows, bins), grid=(count, 2),...  10.6 us
    all_to_all x1, starting transfers between devices, on_device(): received = [lax.all_to_all(sent[0], 'pulse', 0, 0, tiled=True)]  6.55 us
  transfers between devices with their start and end apart: 2, of which 2 were waited for; matrix products, arithmetic and copies ran while one was open for 11% of the time, Pallas kernels for 36%

profile of v3, /device:TPU:15, one launch (start us, length us, event | category | flops | bytes accessed | tf_op | source)
XLA Modules:
  0.0 219.3 jit_solution(2903972839277979645)
XLA Ops:
  0.0 7.6 %pack.3 = f32[16,3,2,128,128]{4,3,2,1,0:T(8,128)} custom-call(f32[2,8,128,1024]{3,2,1,0:T(8,128)} %bitcast.2), custom_call_target="tpu_custom_call" | custom-call | bytes 12582912 | tf_op jit(solution)/shard_map/pack/pallas_call | solution.py:112
  7.6 6.6 %all-to-all-start.1 = ((f32[16,3,2,128,128]{4,3,2,1,0:T(8,128)}), f32[16,3,2,128,128]{4,3,2,1,0:T(8,128)}, u32[]{:S(2)}, u32[]{:S(2)}) async-start(f32[16,3,2,128,128]{4,3,2,1,0:T(8,128)} %pack.3), calls=%async_computation.1 | async-start | bytes 12582912 | tf_op jit(solution)/shard_map/all_to_all | solution.py:466
  14.2 3.0 %pack.2 = f32[16,1,2,128,128]{4,3,2,1,0:T(8,128)} custom-call(f32[2,8,128,1024]{3,2,1,0:T(8,128)} %bitcast.3), custom_call_target="tpu_custom_call" | custom-call | bytes 4194304 | tf_op jit(solution)/shard_map/pack/pallas_call | solution.py:112
  17.1 0.8 dynamic-slice_add_fusion
  17.9 0.1 add.112
  18.0 11.4 %fusion.1.shift_ref = s32[16,128,128]{2,1,0:T(8,128)} fusion(s32[16,128]{1,0:T(8,128)S(1)} %get-tuple-element.12, s32[128]{0:T(128)S(1)} %add.112, s32[16,128]{1,0:T(8,128)S(1)} %get-tuple-element.13, s32[128]{0:T(128)S(1)} %get-tuple-element.10, s32[16,128]{1,0:T(8,128)S(1)} %get-tuple-element.11), kind=kLoop, calls=%fused_computation.4 | loop fusion | flops 2097152 | bytes 1074176 | tf_op jit(solution)/shard_map/sub | solution.py:192
  29.4 11.5 %convert_divide_fusion.fraction_ref = f32[16,128,128]{2,1,0:T(8,128)} fusion(f32[128]{0:T(128)S(1)} %get-tuple-element.9, s32[128]{0:T(128)S(1)} %add.112, s32[16,128]{1,0:T(8,128)S(1)} %get-tuple-element.13, s32[128]{0:T(128)S(1)} %get-tuple-element.10, s32[16,128]{1,0:T(8,128)S(1)} %get-tuple-element.11), kind=kLoop, calls=%fused_computation.1 | loop fusion | flops 2883584 | bytes 1066496 | tf_op jit(solution)/shard_map/div | solution.py:191
  40.9 41.7 %weights.1.weight_ref = f32[16,216,8,128]{3,2,1,0:T(8,128)} custom-call(s32[16,128,128]{2,1,0:T(8,128)} %fusion.1.shift_ref, f32[16,128,128]{2,1,0:T(8,128)} %convert_divide_fusion.fraction_ref), custom_call_target="tpu_custom_call" | custom-call | flops 838860800 | bytes 67108864 | tf_op jit(solution)/shard_map/weights/pallas_call | solution.py:195
  82.6 69.0 %all-to-all-done.1.recv_ref = f32[16,3,2,128,128]{4,3,2,1,0:T(8,128)} async-done(((f32[16,3,2,128,128]{4,3,2,1,0:T(8,128)}), f32[16,3,2,128,128]{4,3,2,1,0:T(8,128)}, u32[]{:S(2)}, u32[]{:S(2)}) %all-to-all-start.1) | async-done | bytes 6291488 | tf_op jit(solution)/shard_map/all_to_all | solution.py:466
  151.6 4.9 %all-to-all-start = ((f32[16,1,2,128,128]{4,3,2,1,0:T(8,128)}), f32[16,1,2,128,128]{4,3,2,1,0:T(8,128)S(1)}, u32[]{:S(2)}, u32[]{:S(2)}) async-start(f32[16,1,2,128,128]{4,3,2,1,0:T(8,128)} %pack.2), calls=%async_computation | async-start | bytes 4194304 | tf_op jit(solution)/shard_map/all_to_all | solution.py:469
  156.5 0.7 fusion.10.scale_ref
  157.2 33.6 %finish.2.rest_0_ = f32[2,8,64,2048]{3,2,1,0:T(8,128)} custom-call(f32[16,3,2,128,128]{4,3,2,1,0:T(8,128)} %all-to-all-done.1.recv_ref, f32[16,216,8,128]{3,2,1,0:T(8,128)} %weights.1.weight_ref, bf16[16,2,2,256,256]{4,3,2,1,0:T(8,128)(2,1)} %constant.64.clone.turn_ref, f32[1,2048]{1,0:T(1,128)} %fusion.10.scale_ref), custom_call_target="tpu_custom_call" | custom-call | flops 4831838208 | bytes 50331648 | tf_op jit(solution)/shard_map/finish/pallas_call | solution.py:432
  190.8 13.1 %all-to-all-done.recv_ref = f32[16,1,2,128,128]{4,3,2,1,0:T(8,128)S(1)} async-done(((f32[16,1,2,128,128]{4,3,2,1,0:T(8,128)}), f32[16,1,2,128,128]{4,3,2,1,0:T(8,128)S(1)}, u32[]{:S(2)}, u32[]{:S(2)}) %all-to-all-start) | async-done | bytes 2097184 | tf_op jit(solution)/shard_map/all_to_all | solution.py:469
  203.9 0.0 copy-start
  203.9 1.3 copy-done
  205.2 14.0 %finish.3 = f32[2,8,64,2048]{3,2,1,0:T(8,128)} custom-call(f32[16,1,2,128,128]{4,3,2,1,0:T(8,128)} %copy-done, f32[16,216,8,128]{3,2,1,0:T(8,128)} %weights.1.weight_ref, bf16[16,2,2,256,256]{4,3,2,1,0:T(8,128)(2,1)} %constant.64.clone.turn_ref, f32[1,2048]{1,0:T(1,128)} %fusion.10.scale_ref, ...), custom_call_target="tpu_custom_call", output_to_operand_aliasing={{}: (4, {})} | custom-call | flops 1610612736 | bytes 41943040 | tf_op jit(solution)/shard_map/finish/pallas_call | solution.py:432
  (4 shorter events, 0.0 us)
Async XLA Ops:
  7.6 144.0 %all-to-all-start.1 = ((f32[16,3,2,128,128]{4,3,2,1,0:T(8,128)}), f32[16,3,2,128,128]{4,3,2,1,0:T(8,128)}, u32[]{:S(2)}, u32[]{:S(2)}) async-start(f32[16,3,2,128,128]{4,3,2,1,0:T(8,128)} %pack.3), calls=%async_computation.1 | async-start | bytes 12582912 | tf_op jit(solution)/shard_map/all_to_all | solution.py:466
  151.6 52.3 %all-to-all-start = ((f32[16,1,2,128,128]{4,3,2,1,0:T(8,128)}), f32[16,1,2,128,128]{4,3,2,1,0:T(8,128)S(1)}, u32[]{:S(2)}, u32[]{:S(2)}) async-start(f32[16,1,2,128,128]{4,3,2,1,0:T(8,128)} %pack.2), calls=%async_computation | async-start | bytes 4194304 | tf_op jit(solution)/shard_map/all_to_all | solution.py:469
  203.9 1.3 copy-start

commit v4 on v3

--- a/solution.py
+++ b/solution.py
@@ -86,37 +86,60 @@
     return both.reshape(MINOR, 2, 2, 2 * MAJOR, 2 * MAJOR)
 
 
-def pack_body(rows, bins, echo_ref, out_ref):
+def pack_body(rows, bins, first, pieces, echo_ref, out_ref, taken, ready, taking, leaving):
     held = echo_ref.shape[2]
     depth = held // MINOR
     lane = lax.broadcasted_iota(jnp.int32, (8, LANES), 1) // bins
-    for column in range(BINS // LANES):
-        for group in range(held // 8):
-            taken = [
-                echo_ref[0, row, pl.ds(8 * group, 8), pl.ds(column * LANES, LANES)] for row in range(rows)
-            ]
-            to = pl.ds(8 * group % MINOR * depth + 8 * group // MINOR, 8, stride=depth)
-            for dest in range(rows):
-                value = None
-                for row in range(rows):
-                    turn = (row - dest) * bins % LANES
-                    moved = pltpu.roll(taken[row], turn, 1) if turn else taken[row]
-                    value = moved if value is None else jnp.where(lane == row, moved, value)
-                out_ref[column * rows + dest, 0, 0, to, :] = value
+
+    def take(piece):
+        source = echo_ref.at[piece % 2, pl.ds((first + piece // 2) * rows, rows)]
+        return pltpu.make_async_copy(source, taken.at[piece], taking.at[piece])
+
+    def leave(piece):
+        return pltpu.make_async_copy(ready.at[piece], out_ref.at[:, piece // 2, piece % 2], leaving.at[piece])
+
+    for piece in range(pieces):
+        take(piece).start()
+
+    @pl.loop(0, pieces)
+    def _(piece):
+        take(piece).wait()
+        for column in range(BINS // LANES):
+            for group in range(held // 8):
+                values = [
+                    taken[piece, row, pl.ds(8 * group, 8), pl.ds(column * LANES, LANES)] for row in range(rows)
+                ]
+                to = pl.ds(8 * group % MINOR * depth + 8 * group // MINOR, 8, stride=depth)
+                for dest in range(rows):
+                    value = None
+                    for row in range(rows):
+                        turn = (row - dest) * bins % LANES
+                        moved = pltpu.roll(values[row], turn, 1) if turn else values[row]
+                        value = moved if value is None else jnp.where(lane == row, moved, value)
+                    ready[piece, column * rows + dest, to, :] = value
+        leave(piece).start()
+
+    @pl.loop(0, pieces)
+    def _(piece):
+        leave(piece).wait()
 
 
 def pack(echo, first, count, devices):
     bins = BINS // devices
     rows = LANES // bins
     held = echo.shape[2]
+    pieces = 2 * count
     return pl.pallas_call(
-        functools.partial(pack_body, rows, bins),
-        grid=(count, 2),
-        in_specs=[
-            pl.BlockSpec((1, rows, held, BINS), lambda u, part: (part, u + first, 0, 0)),
+        functools.partial(pack_body, rows, bins, first, pieces),
+        in_specs=[pl.BlockSpec(memory_space=pl.ANY)],
+        out_specs=pl.BlockSpec(memory_space=pl.ANY),
+        out_shape=jax.ShapeDtypeStruct((devices, count, 2, held, LANES), jnp.float32),
+        scratch_shapes=[
+            pltpu.VMEM((pieces, rows, held, BINS), jnp.float32),
+            pltpu.VMEM((pieces, devices, held, LANES), jnp.float32),
+            pltpu.SemaphoreType.DMA((pieces,)),
+            pltpu.SemaphoreType.DMA((pieces,)),
         ],
-        out_specs=pl.BlockSpec((devices, 1, 1, held, LANES), lambda u, part: (0, u, part, 0, 0)),
-        out_shape=jax.ShapeDtypeStruct((devices, count, 2, held, LANES), jnp.float32),
         compiler_params=pltpu.CompilerParams(vmem_limit_bytes=56 * 2**20),
         cost_estimate=pl.CostEstimate(
             flops=0, bytes_accessed=16 * devices * count * held * LANES, transcendentals=0
@@ -337,20 +360,22 @@
             start, offsets = table[block]
             sums = {}
             for index, e in enumerate(offsets):
-                both = weight_ref[weight_at, start + index]
-                ahead = pltpu.roll(both, bins, 1)
-                behind = ahead if 2 * bins == LANES else pltpu.roll(both, LANES - bins, 1)
-                weight = (jnp.where(first_parity, both, ahead), jnp.where(first_parity, behind, both))
+                weight = weight_ref[weight_at, start + index]
+                weight = (weight, pltpu.roll(weight, bins, 1))
                 row = q1 - e + PAD
                 for part in range(2):
                     for unit in range(count):
                         sample = spread[row, part, unit, pl.ds(8 * block, 8), :]
-                        for parity in range(2):
-                            term = weight[parity] * sample
-                            key = (parity, part, unit)
+                        for turn in range(2):
+                            term = weight[turn] * sample
+                            key = (turn, part, unit)
                             sums[key] = sums[key] + term if key in sums else term
-            for (parity, part, unit), value in sums.items():
-                pairs[parity, pl.ds(part * MAJOR + 8 * block, 8), pl.ds(unit * LANES, LANES)] = value
+            for part in range(2):
+                for unit in range(count):
+                    own, other = sums[0, part, unit], sums[1, part, unit]
+                    at = (pl.ds(part * MAJOR + 8 * block, 8), pl.ds(unit * LANES, LANES))
+                    pairs[(0,) + at] = jnp.where(first_parity, own, other)
+                    pairs[(1,) + at] = jnp.where(first_parity, other, own)
 
     def leave(unit, part):
         return pltpu.make_async_copy(
@@ -445,7 +470,7 @@
         ]
         + ahead,
         input_output_aliases={} if base is None else {4: 0},
-        compiler_params=pltpu.CompilerParams(vmem_limit_bytes=(54 if close else 58) * 2**20),
+        compiler_params=pltpu.CompilerParams(vmem_limit_bytes=(48 if close else 58) * 2**20),
         cost_estimate=pl.CostEstimate(
             flops=count * 32 * 6 * 256 * 256 * 128, bytes_accessed=(36 + 4 * count) * 2**20, transcendentals=0
         ),

time: 220 us -> 214 us (0.973)
  Pallas kernels: 99.8 us -> 95 us
    pallas_call x2, Pallas kernels: 10.6 us -> 7.89 us  [pack(): pl.pallas_call(functools.partial(pack_body, rows, bins, first, pieces), i...]
  transfers between devices with their start and end apart: 2 -> 2, of which waited for: 2 -> 2; matrix products, arithmetic and copies ran while one was open for 11% -> 11% of each run, Pallas kernels for 36% -> 37%
where the time goes in v4:
time: 214 us; the launch traced here: 213 us
  Pallas kernels  95 us (44%)
  waiting for transfers between devices  82.1 us (38%)
  other arithmetic  24.4 us (11%)
  starting transfers between devices  11.5 us (5%)
    all_to_all x1, waiting for transfers between devices, on_device(): received = [lax.all_to_all(sent[0], 'pulse', 0, 0, tiled=True)]  69 us
    pallas_call x2, Pallas kernels, finish(): pl.pallas_call(functools.partial(main_body, first, count, rows, bins, bas...  45.4 us
    pallas_call x1, Pallas kernels, weights(): pl.pallas_call(functools.partial(weight_body, bins), grid=(MINOR,), in_sp...  41.7 us
    all_to_all x1, waiting for transfers between devices, on_device(): received.append(lax.all_to_all(later, 'pulse', 0, 0, tiled=True))  13.1 us
    div x1, other arithmetic, weights(): (numerator - cell_floor * denominator).astype(jnp.float32)  11.5 us
    sub x1, other arithmetic, weights(): shift = cell_floor - 2 * slow  11.4 us
    pallas_call x2, Pallas kernels, pack(): pl.pallas_call(functools.partial(pack_body, rows, bins, first, pieces), i...  7.89 us
    all_to_all x1, starting transfers between devices, on_device(): received = [lax.all_to_all(sent[0], 'pulse', 0, 0, tiled=True)]  6.57 us
  transfers between devices with their start and end apart: 2, of which 2 were waited for; matrix products, arithmetic and copies ran while one was open for 11% of the time, Pallas kernels for 37%

profile of v4, /device:TPU:15, one launch (start us, length us, event | category | flops | bytes accessed | tf_op | source)
XLA Modules:
  0.0 213.2 jit_solution(7034422150092289550)
XLA Ops:
  0.0 4.9 %pack.3 = f32[16,3,2,128,128]{4,3,2,1,0:T(8,128)} custom-call(f32[2,8,128,1024]{3,2,1,0:T(8,128)} %bitcast.2), custom_call_target="tpu_custom_call" | custom-call | bytes 12582912 | tf_op jit(solution)/shard_map/pack/pallas_call | solution.py:132
  5.0 6.6 %all-to-all-start.1 = ((f32[16,3,2,128,128]{4,3,2,1,0:T(8,128)}), f32[16,3,2,128,128]{4,3,2,1,0:T(8,128)}, u32[]{:S(2)}, u32[]{:S(2)}) async-start(f32[16,3,2,128,128]{4,3,2,1,0:T(8,128)} %pack.3), calls=%async_computation.1 | async-start | bytes 12582912 | tf_op jit(solution)/shard_map/all_to_all | solution.py:491
  11.5 2.9 %pack.2 = f32[16,1,2,128,128]{4,3,2,1,0:T(8,128)} custom-call(f32[2,8,128,1024]{3,2,1,0:T(8,128)} %bitcast.3), custom_call_target="tpu_custom_call" | custom-call | bytes 4194304 | tf_op jit(solution)/shard_map/pack/pallas_call | solution.py:132
  14.5 0.8 dynamic-slice_add_fusion
  15.3 0.1 add.112
  15.4 11.4 %fusion.1.shift_ref = s32[16,128,128]{2,1,0:T(8,128)} fusion(s32[16,128]{1,0:T(8,128)S(1)} %get-tuple-element.12, s32[128]{0:T(128)S(1)} %add.112, s32[16,128]{1,0:T(8,128)S(1)} %get-tuple-element.13, s32[128]{0:T(128)S(1)} %get-tuple-element.10, s32[16,128]{1,0:T(8,128)S(1)} %get-tuple-element.11), kind=kLoop, calls=%fused_computation.4 | loop fusion | flops 2097152 | bytes 1074176 | tf_op jit(solution)/shard_map/sub | solution.py:215
  26.8 11.5 %convert_divide_fusion.fraction_ref = f32[16,128,128]{2,1,0:T(8,128)} fusion(f32[128]{0:T(128)S(1)} %get-tuple-element.9, s32[128]{0:T(128)S(1)} %add.112, s32[16,128]{1,0:T(8,128)S(1)} %get-tuple-element.13, s32[128]{0:T(128)S(1)} %get-tuple-element.10, s32[16,128]{1,0:T(8,128)S(1)} %get-tuple-element.11), kind=kLoop, calls=%fused_computation.1 | loop fusion | flops 2883584 | bytes 1066496 | tf_op jit(solution)/shard_map/div | solution.py:214
  38.3 41.7 %weights.1.weight_ref = f32[16,216,8,128]{3,2,1,0:T(8,128)} custom-call(s32[16,128,128]{2,1,0:T(8,128)} %fusion.1.shift_ref, f32[16,128,128]{2,1,0:T(8,128)} %convert_divide_fusion.fraction_ref), custom_call_target="tpu_custom_call" | custom-call | flops 838860800 | bytes 67108864 | tf_op jit(solution)/shard_map/weights/pallas_call | solution.py:218
  79.9 69.0 %all-to-all-done.1.recv_ref = f32[16,3,2,128,128]{4,3,2,1,0:T(8,128)} async-done(((f32[16,3,2,128,128]{4,3,2,1,0:T(8,128)}), f32[16,3,2,128,128]{4,3,2,1,0:T(8,128)}, u32[]{:S(2)}, u32[]{:S(2)}) %all-to-all-start.1) | async-done | bytes 6291488 | tf_op jit(solution)/shard_map/all_to_all | solution.py:491
  148.9 4.9 %all-to-all-start = ((f32[16,1,2,128,128]{4,3,2,1,0:T(8,128)}), f32[16,1,2,128,128]{4,3,2,1,0:T(8,128)S(1)}, u32[]{:S(2)}, u32[]{:S(2)}) async-start(f32[16,1,2,128,128]{4,3,2,1,0:T(8,128)} %pack.2), calls=%async_computation | async-start | bytes 4194304 | tf_op jit(solution)/shard_map/all_to_all | solution.py:494
  153.8 0.7 fusion.10.scale_ref
  154.6 0.0 copy-start
  154.6 33.6 %finish.2.rest_0_ = f32[2,8,64,2048]{3,2,1,0:T(8,128)} custom-call(f32[16,3,2,128,128]{4,3,2,1,0:T(8,128)} %all-to-all-done.1.recv_ref, f32[16,216,8,128]{3,2,1,0:T(8,128)} %weights.1.weight_ref, bf16[16,2,2,256,256]{4,3,2,1,0:T(8,128)(2,1)} %constant.64.clone.turn_ref, f32[1,2048]{1,0:T(1,128)} %fusion.10.scale_ref), custom_call_target="tpu_custom_call" | custom-call | flops 4831838208 | bytes 50331648 | tf_op jit(solution)/shard_map/finish/pallas_call | solution.py:457
  188.1 13.1 %all-to-all-done.recv_ref = f32[16,1,2,128,128]{4,3,2,1,0:T(8,128)S(1)} async-done(((f32[16,1,2,128,128]{4,3,2,1,0:T(8,128)}), f32[16,1,2,128,128]{4,3,2,1,0:T(8,128)S(1)}, u32[]{:S(2)}, u32[]{:S(2)}) %all-to-all-start) | async-done | bytes 2097184 | tf_op jit(solution)/shard_map/all_to_all | solution.py:494
  201.3 0.0 copy-done
  201.3 11.8 %finish.3 = f32[2,8,64,2048]{3,2,1,0:T(8,128)} custom-call(f32[16,1,2,128,128]{4,3,2,1,0:T(8,128)S(1)} %all-to-all-done.recv_ref, f32[16,216,8,128]{3,2,1,0:T(8,128)} %weights.1.weight_ref, bf16[16,2,2,256,256]{4,3,2,1,0:T(8,128)(2,1)} %constant.64.clone.turn_ref, f32[1,2048]{1,0:T(1,128)S(1)} %copy-done, ...), custom_call_target="tpu_custom_call", output_to_operand_aliasing={{}: (4, {})} | custom-call | flops 1610612736 | bytes 41943040 | tf_op jit(solution)/shard_map/finish/pallas_call | solution.py:457
  (4 shorter events, 0.0 us)
Async XLA Ops:
  5.0 144.0 %all-to-all-start.1 = ((f32[16,3,2,128,128]{4,3,2,1,0:T(8,128)}), f32[16,3,2,128,128]{4,3,2,1,0:T(8,128)}, u32[]{:S(2)}, u32[]{:S(2)}) async-start(f32[16,3,2,128,128]{4,3,2,1,0:T(8,128)} %pack.3), calls=%async_computation.1 | async-start | bytes 12582912 | tf_op jit(solution)/shard_map/all_to_all | solution.py:491
  148.9 52.3 %all-to-all-start = ((f32[16,1,2,128,128]{4,3,2,1,0:T(8,128)}), f32[16,1,2,128,128]{4,3,2,1,0:T(8,128)S(1)}, u32[]{:S(2)}, u32[]{:S(2)}) async-start(f32[16,1,2,128,128]{4,3,2,1,0:T(8,128)} %pack.2), calls=%async_computation | async-start | bytes 4194304 | tf_op jit(solution)/shard_map/all_to_all | solution.py:494
  154.6 46.7 %copy-start = (f32[1,2048]{1,0:T(1,128)S(1)}, f32[1,2048]{1,0:T(1,128)}, u32[]{:S(2)}) copy-start(f32[1,2048]{1,0:T(1,128)} %fusion.10.scale_ref) | copy-start | bytes 24580

commit v5 on v4

--- a/solution.py
+++ b/solution.py
@@ -18,6 +18,8 @@
 PAD = 10
 BLOCKS = MAJOR // 8
 LANES = 128
+AHEAD = 6
+CUTS = 2
 
 BETA_KB = math.pi * math.sqrt(35.2)
 
@@ -98,12 +100,17 @@
     def leave(piece):
         return pltpu.make_async_copy(ready.at[piece], out_ref.at[:, piece // 2, piece % 2], leaving.at[piece])
 
-    for piece in range(pieces):
+    for piece in range(min(AHEAD, pieces)):
         take(piece).start()
 
     @pl.loop(0, pieces)
     def _(piece):
         take(piece).wait()
+
+        @pl.when(piece + AHEAD < pieces)
+        def _():
+            take(piece + AHEAD).start()
+
         for column in range(BINS // LANES):
             for group in range(held // 8):
                 values = [
@@ -291,8 +298,6 @@
     if has_base:
         rest = rest[1:]
     out_ref, spread, pairs, mids, tall, wide, sem = rest[:7]
-    q1 = pl.program_id(0)
-    before = jnp.maximum(q1 - 1, 0)
     if close:
         weight_far, turn_far = weight_ref, turn_ref
         weight_ref, turn_ref, fetched = rest[7:]
@@ -303,16 +308,13 @@
         def fetch_turn(q):
             return pltpu.make_async_copy(turn_far.at[q], turn_ref.at[q], fetched.at[1, q])
 
-        @pl.when(q1 == 0)
-        def _():
-            for q in range(MINOR):
-                fetch_weight(q).start()
-                fetch_turn(q).start()
+        for q in range(MINOR):
+            fetch_weight(q).start()
+            fetch_turn(q).start()
 
     devices, depth = recv_ref.shape[0], recv_ref.shape[3] // MINOR
 
-    @pl.when(q1 == 0)
-    def _():
+    def begin():
         for unit in range(count):
             for part in range(2):
                 @pl.loop(0, MINOR)
@@ -326,7 +328,7 @@
 
                 extend(lambda row: spread[row, part, unit], keep)
 
-    def combine():
+    def combine(before):
         turn_at = before if close else 0
         dot = functools.partial(jnp.dot, preferred_element_type=jnp.float32)
         width = count * LANES
@@ -341,18 +343,16 @@
             else:
                 mids[before, parity] = dot(turn_high, high) + (dot(turn_high, low) + dot(turn_low, high))
 
-    if close:
-        @pl.when(q1 < MINOR)
-        def _():
+    def step(q1):
+        before = jnp.maximum(q1 - 1, 0)
+        if close:
             fetch_weight(q1).wait()
 
-        @pl.when(q1 != 1)
-        def _():
-            fetch_turn(before).wait()
-
-    @pl.when(q1 < MINOR)
-    def _():
-        combine()
+            @pl.when(q1 != 1)
+            def _():
+                fetch_turn(before).wait()
+
+        combine(before)
         weight_at = q1 if close else 0
         table, _ = windows()
         first_parity = lax.broadcasted_iota(jnp.int32, (8, LANES), 1) // bins % 2 == 0
@@ -377,16 +377,20 @@
                     pairs[(0,) + at] = jnp.where(first_parity, own, other)
                     pairs[(1,) + at] = jnp.where(first_parity, other, own)
 
-    def leave(unit, part):
+    span = PULSES // CUTS
+
+    def leave(unit, part, cut):
+        at = pl.ds(pl.multiple_of(cut * span, span), span)
         return pltpu.make_async_copy(
-            wide.at[part],
-            out_ref.at[part, pl.ds((first + unit) * rows, rows)],
-            sem.at[unit, part],
+            wide.at[part, :, :, at],
+            out_ref.at[part, pl.ds((first + unit) * rows, rows), :, at],
+            sem.at[unit, part, cut],
         )
 
-    @pl.when(q1 == MINOR)
-    def _():
-        combine()
+    def end():
+        if close:
+            fetch_turn(MINOR - 1).wait()
+        combine(MINOR - 1)
         for unit in range(count):
             across = pl.ds(unit * LANES, LANES)
 
@@ -407,21 +411,30 @@
                         tall[part, n1, pl.ds(pl.multiple_of(8 * block, 8), 8), :] = value[part]
 
             for part in range(2):
-                if unit:
-                    leave(unit - 1, part).wait()
-
-                @pl.loop(0, 4)
-                def _(group):
-                    for member in range(4):
-                        n1 = 4 * group + member
+                @pl.loop(0, CUTS)
+                def _(cut):
+                    if unit:
+                        leave(unit - 1, part, cut).wait()
+                    for member in range(16 // CUTS):
+                        n1 = cut * (16 // CUTS) + member
                         at = pl.ds(pl.multiple_of(n1 * LANES, LANES), LANES)
                         turned = jnp.transpose(tall[part, n1]) * scale_ref[pl.ds(0, 1), at]
                         for row in range(rows):
                             wide[part, row, :, at] = turned[row * bins : (row + 1) * bins]
-
-                leave(unit, part).start()
+                    leave(unit, part, cut).start()
         for part in range(2):
-            leave(count - 1, part).wait()
+            for cut in range(CUTS):
+                leave(count - 1, part, cut).wait()
+
+    if close:
+        begin()
+        pl.loop(0, MINOR)(step)
+        end()
+    else:
+        now = pl.program_id(0)
+        pl.when(now == 0)(begin)
+        pl.when(now < MINOR)(lambda: step(now))
+        pl.when(now == MINOR)(end)
 
 
 def finish(recv, weight, turn, scale, base, first, total):
@@ -442,7 +455,7 @@
             pl.BlockSpec((1, entries, 8, LANES), lambda q: (jnp.minimum(q, MINOR - 1), 0, 0, 0)),
             pl.BlockSpec((1, 2, 2, 2 * MAJOR, 2 * MAJOR), lambda q: (jnp.maximum(q - 1, 0), 0, 0, 0, 0)),
         ]
-    in_specs.append(pl.BlockSpec((1, PULSES), lambda q: (0, 0)))
+    in_specs.append(pl.BlockSpec((1, PULSES), (lambda: (0, 0)) if close else (lambda q: (0, 0))))
     args = [recv, weight, turn, scale]
     if base is not None:
         in_specs.append(pl.BlockSpec(memory_space=pl.ANY))
@@ -456,7 +469,7 @@
         ]
     return pl.pallas_call(
         functools.partial(main_body, first, count, rows, bins, base is not None, close),
-        grid=(MINOR + 1,),
+        grid=() if close else (MINOR + 1,),
         in_specs=in_specs,
         out_specs=pl.BlockSpec(memory_space=pl.ANY),
         out_shape=jax.ShapeDtypeStruct((2, total, bins, PULSES), jnp.float32),
@@ -466,7 +479,7 @@
             pltpu.VMEM((MINOR, 2, 2 * MAJOR, count * LANES), jnp.float32),
             pltpu.VMEM((2, 16, MAJOR, LANES), jnp.float32),
             pltpu.VMEM((2, rows, bins, PULSES), jnp.float32),
-            pltpu.SemaphoreType.DMA((count, 2)),
+            pltpu.SemaphoreType.DMA((count, 2, CUTS)),
         ]
         + ahead,
         input_output_aliases={} if base is None else {4: 0},

time: 214 us -> 213 us (level)
  transfers between devices with their start and end apart: 2 -> 2, of which waited for: 2 -> 2; matrix products, arithmetic and copies ran while one was open for 11% -> 12% of each run, Pallas kernels for 37% -> 36%
where the time goes in v5:
time: 213 us
  Pallas kernels  93.6 us (44%)
  waiting for transfers between devices  83.1 us (39%)
  other arithmetic  24.4 us (11%)
  starting transfers between devices  11.5 us (5%)
    all_to_all x1, waiting for transfers between devices, on_device(): received = [lax.all_to_all(sent[0], 'pulse', 0, 0, tiled=True)]  69 us
    pallas_call x2, Pallas kernels, finish(): pl.pallas_call(functools.partial(main_body, first, count, rows, bins, bas...  44 us
    pallas_call x1, Pallas kernels, weights(): pl.pallas_call(functools.partial(weight_body, bins), grid=(MINOR,), in_sp...  41.7 us
    all_to_all x1, waiting for transfers between devices, on_device(): received.append(lax.all_to_all(later, 'pulse', 0, 0, tiled=True))  14.1 us
    div x1, other arithmetic, weights(): (numerator - cell_floor * denominator).astype(jnp.float32)  11.5 us
    sub x1, other arithmetic, weights(): shift = cell_floor - 2 * slow  11.4 us
    pallas_call x2, Pallas kernels, pack(): pl.pallas_call(functools.partial(pack_body, rows, bins, first, pieces), i...  7.9 us
    all_to_all x1, starting transfers between devices, on_device(): received = [lax.all_to_all(sent[0], 'pulse', 0, 0, tiled=True)]  6.57 us
  transfers between devices with their start and end apart: 2, of which 2 were waited for; matrix products, arithmetic and copies ran while one was open for 12% of the time, Pallas kernels for 36%

profile of v5, /device:TPU:15, one launch (start us, length us, event | category | flops | bytes accessed | tf_op | source)
XLA Modules:
  0.0 212.8 jit_solution(6659175773038760213)
XLA Ops:
  0.0 4.9 %pack.3 = f32[16,3,2,128,128]{4,3,2,1,0:T(8,128)} custom-call(f32[2,8,128,1024]{3,2,1,0:T(8,128)} %bitcast.2), custom_call_target="tpu_custom_call" | custom-call | bytes 12582912 | tf_op jit(solution)/shard_map/pack/pallas_call | solution.py:139
  5.0 6.6 %all-to-all-start.1 = ((f32[16,3,2,128,128]{4,3,2,1,0:T(8,128)}), f32[16,3,2,128,128]{4,3,2,1,0:T(8,128)}, u32[]{:S(2)}, u32[]{:S(2)}) async-start(f32[16,3,2,128,128]{4,3,2,1,0:T(8,128)} %pack.3), calls=%async_computation.1 | async-start | bytes 12582912 | tf_op jit(solution)/shard_map/all_to_all | solution.py:504
  11.5 3.0 %pack.2 = f32[16,1,2,128,128]{4,3,2,1,0:T(8,128)} custom-call(f32[2,8,128,1024]{3,2,1,0:T(8,128)} %bitcast.3), custom_call_target="tpu_custom_call" | custom-call | bytes 4194304 | tf_op jit(solution)/shard_map/pack/pallas_call | solution.py:139
  14.5 0.8 dynamic-slice_add_fusion
  15.3 0.1 add.112
  15.4 11.4 %fusion.1.shift_ref = s32[16,128,128]{2,1,0:T(8,128)} fusion(s32[16,128]{1,0:T(8,128)S(1)} %get-tuple-element.12, s32[128]{0:T(128)S(1)} %add.112, s32[16,128]{1,0:T(8,128)S(1)} %get-tuple-element.13, s32[128]{0:T(128)S(1)} %get-tuple-element.10, s32[16,128]{1,0:T(8,128)S(1)} %get-tuple-element.11), kind=kLoop, calls=%fused_computation.4 | loop fusion | flops 2097152 | bytes 1074176 | tf_op jit(solution)/shard_map/sub | solution.py:222
  26.8 11.5 %convert_divide_fusion.fraction_ref = f32[16,128,128]{2,1,0:T(8,128)} fusion(f32[128]{0:T(128)S(1)} %get-tuple-element.9, s32[128]{0:T(128)S(1)} %add.112, s32[16,128]{1,0:T(8,128)S(1)} %get-tuple-element.13, s32[128]{0:T(128)S(1)} %get-tuple-element.10, s32[16,128]{1,0:T(8,128)S(1)} %get-tuple-element.11), kind=kLoop, calls=%fused_computation.1 | loop fusion | flops 2883584 | bytes 1066496 | tf_op jit(solution)/shard_map/div | solution.py:221
  38.3 41.7 %weights.1.weight_ref = f32[16,216,8,128]{3,2,1,0:T(8,128)} custom-call(s32[16,128,128]{2,1,0:T(8,128)} %fusion.1.shift_ref, f32[16,128,128]{2,1,0:T(8,128)} %convert_divide_fusion.fraction_ref), custom_call_target="tpu_custom_call" | custom-call | flops 838860800 | bytes 67108864 | tf_op jit(solution)/shard_map/weights/pallas_call | solution.py:225
  79.9 69.0 %all-to-all-done.1.recv_ref = f32[16,3,2,128,128]{4,3,2,1,0:T(8,128)} async-done(((f32[16,3,2,128,128]{4,3,2,1,0:T(8,128)}), f32[16,3,2,128,128]{4,3,2,1,0:T(8,128)}, u32[]{:S(2)}, u32[]{:S(2)}) %all-to-all-start.1) | async-done | bytes 6291488 | tf_op jit(solution)/shard_map/all_to_all | solution.py:504
  148.9 4.9 %all-to-all-start = ((f32[16,1,2,128,128]{4,3,2,1,0:T(8,128)}), f32[16,1,2,128,128]{4,3,2,1,0:T(8,128)S(1)}, u32[]{:S(2)}, u32[]{:S(2)}) async-start(f32[16,1,2,128,128]{4,3,2,1,0:T(8,128)} %pack.2), calls=%async_computation | async-start | bytes 4194304 | tf_op jit(solution)/shard_map/all_to_all | solution.py:507
  153.8 0.7 fusion.10.scale_ref
  154.6 0.0 copy-start
  154.6 32.6 %finish.2.rest_0_ = f32[2,8,64,2048]{3,2,1,0:T(8,128)} custom-call(f32[16,3,2,128,128]{4,3,2,1,0:T(8,128)} %all-to-all-done.1.recv_ref, f32[16,216,8,128]{3,2,1,0:T(8,128)} %weights.1.weight_ref, bf16[16,2,2,256,256]{4,3,2,1,0:T(8,128)(2,1)} %constant.64.clone.turn_ref, f32[1,2048]{1,0:T(1,128)} %fusion.10.scale_ref), custom_call_target="tpu_custom_call" | custom-call | flops 4831838208 | bytes 50331648 | tf_op jit(solution)/shard_map/finish/pallas_call | solution.py:470
  187.2 14.1 %all-to-all-done.recv_ref = f32[16,1,2,128,128]{4,3,2,1,0:T(8,128)S(1)} async-done(((f32[16,1,2,128,128]{4,3,2,1,0:T(8,128)}), f32[16,1,2,128,128]{4,3,2,1,0:T(8,128)S(1)}, u32[]{:S(2)}, u32[]{:S(2)}) %all-to-all-start) | async-done | bytes 2097184 | tf_op jit(solution)/shard_map/all_to_all | solution.py:507
  201.3 0.0 copy-done
  201.3 11.4 %finish.3 = f32[2,8,64,2048]{3,2,1,0:T(8,128)} custom-call(f32[16,1,2,128,128]{4,3,2,1,0:T(8,128)S(1)} %all-to-all-done.recv_ref, f32[16,216,8,128]{3,2,1,0:T(8,128)} %weights.1.weight_ref, bf16[16,2,2,256,256]{4,3,2,1,0:T(8,128)(2,1)} %constant.64.clone.turn_ref, f32[1,2048]{1,0:T(1,128)S(1)} %copy-done, ...), custom_call_target="tpu_custom_call", output_to_operand_aliasing={{}: (4, {})} | custom-call | flops 1610612736 | bytes 41943040 | tf_op jit(solution)/shard_map/finish/pallas_call | solution.py:470
  (4 shorter events, 0.0 us)
Async XLA Ops:
  5.0 144.0 %all-to-all-start.1 = ((f32[16,3,2,128,128]{4,3,2,1,0:T(8,128)}), f32[16,3,2,128,128]{4,3,2,1,0:T(8,128)}, u32[]{:S(2)}, u32[]{:S(2)}) async-start(f32[16,3,2,128,128]{4,3,2,1,0:T(8,128)} %pack.3), calls=%async_computation.1 | async-start | bytes 12582912 | tf_op jit(solution)/shard_map/all_to_all | solution.py:504
  148.9 52.3 %all-to-all-start = ((f32[16,1,2,128,128]{4,3,2,1,0:T(8,128)}), f32[16,1,2,128,128]{4,3,2,1,0:T(8,128)S(1)}, u32[]{:S(2)}, u32[]{:S(2)}) async-start(f32[16,1,2,128,128]{4,3,2,1,0:T(8,128)} %pack.2), calls=%async_computation | async-start | bytes 4194304 | tf_op jit(solution)/shard_map/all_to_all | solution.py:507
  154.6 46.7 %copy-start = (f32[1,2048]{1,0:T(1,128)S(1)}, f32[1,2048]{1,0:T(1,128)}, u32[]{:S(2)}) copy-start(f32[1,2048]{1,0:T(1,128)} %fusion.10.scale_ref) | copy-start | bytes 24580

commit v6 on v5

--- a/solution.py
+++ b/solution.py
@@ -331,15 +331,19 @@
     def combine(before):
         turn_at = before if close else 0
         dot = functools.partial(jnp.dot, preferred_element_type=jnp.float32)
-        width = count * LANES
         for parity in range(2):
             full = pairs[parity]
             high = full.astype(jnp.bfloat16)
             low = (full - high.astype(jnp.float32)).astype(jnp.bfloat16)
             turn_high, turn_low = turn_ref[turn_at, parity, 0], turn_ref[turn_at, parity, 1]
             if count == 1:
-                both = dot(turn_high, jnp.concatenate([high, low], 1))
-                mids[before, parity] = both[:, :width] + (both[:, width:] + dot(turn_low, high))
+                across = functools.partial(
+                    lax.dot_general,
+                    dimension_numbers=(((0,), (1,)), ((), ())),
+                    preferred_element_type=jnp.float32,
+                )
+                both = across(jnp.concatenate([high, low], 1), turn_high)
+                mids[before, parity] = both[:LANES] + (both[LANES:] + across(high, turn_low))
             else:
                 mids[before, parity] = dot(turn_high, high) + (dot(turn_high, low) + dot(turn_low, high))
 
@@ -387,9 +391,41 @@
             sem.at[unit, part, cut],
         )
 
+    def depart(row):
+        return pltpu.make_async_copy(
+            wide.at[:, row], out_ref.at[:, first * rows + row], sem.at[0, 0, row % CUTS]
+        )
+
+    def end_close():
+        fetch_turn(MINOR - 1).wait()
+        combine(MINOR - 1)
+        for row in range(rows):
+            if row >= CUTS:
+                depart(row - CUTS).wait()
+
+            @pl.loop(0, bins // 8, unroll=2)
+            def _(group):
+                here = pl.ds(pl.multiple_of(group * 8, 8), 8)
+
+                def load(parity, q):
+                    return tuple(
+                        mids[q, parity, pl.ds(pl.multiple_of(row * bins + group * 8, 8), 8), pl.ds(part * LANES, LANES)]
+                        for part in range(2)
+                    )
+
+                even = dft16(functools.partial(load, 0))
+                odd = dft16(functools.partial(load, 1))
+                for n1 in range(16):
+                    at = pl.ds(n1 * LANES, LANES)
+                    value = plus(even[(n1 - 8) % 16], times(odd[(n1 - 8) % 16], n1 - 8, 32))
+                    for part in range(2):
+                        wide[part, row, here, at] = value[part] * scale_ref[pl.ds(0, 1), at]
+
+            depart(row).start()
+        for row in range(max(rows - CUTS, 0), rows):
+            depart(row).wait()
+
     def end():
-        if close:
-            fetch_turn(MINOR - 1).wait()
         combine(MINOR - 1)
         for unit in range(count):
             across = pl.ds(unit * LANES, LANES)
@@ -429,7 +465,7 @@
     if close:
         begin()
         pl.loop(0, MINOR)(step)
-        end()
+        end_close()
     else:
         now = pl.program_id(0)
         pl.when(now == 0)(begin)
@@ -476,7 +512,7 @@
         scratch_shapes=[
             pltpu.VMEM((MINOR + 2 * PAD, 2, count, MAJOR, LANES), jnp.float32),
             pltpu.VMEM((2, 2 * MAJOR, count * LANES), jnp.float32),
-            pltpu.VMEM((MINOR, 2, 2 * MAJOR, count * LANES), jnp.float32),
+            pltpu.VMEM((MINOR, 2) + ((LANES, 2 * MAJOR) if close else (2 * MAJOR, count * LANES)), jnp.float32),
             pltpu.VMEM((2, 16, MAJOR, LANES), jnp.float32),
             pltpu.VMEM((2, rows, bins, PULSES), jnp.float32),
             pltpu.SemaphoreType.DMA((count, 2, CUTS)),

time: 213 us -> 213 us (level)
  no operation moved by 1% of the time
where the time goes in v6:
time: 213 us; the launch traced here: 212 us
  Pallas kernels  93.3 us (44%)
  waiting for transfers between devices  83.1 us (39%)
  other arithmetic  24.4 us (11%)
  starting transfers between devices  11.5 us (5%)
    all_to_all x1, waiting for transfers between devices, on_device(): received = [lax.all_to_all(sent[0], 'pulse', 0, 0, tiled=True)]  69 us
    pallas_call x2, Pallas kernels, finish(): pl.pallas_call(functools.partial(main_body, first, count, rows, bins, bas...  43.7 us
    pallas_call x1, Pallas kernels, weights(): pl.pallas_call(functools.partial(weight_body, bins), grid=(MINOR,), in_sp...  41.7 us
    all_to_all x1, waiting for transfers between devices, on_device(): received.append(lax.all_to_all(later, 'pulse', 0, 0, tiled=True))  14.1 us
    div x1, other arithmetic, weights(): (numerator - cell_floor * denominator).astype(jnp.float32)  11.5 us
    sub x1, other arithmetic, weights(): shift = cell_floor - 2 * slow  11.4 us
    pallas_call x2, Pallas kernels, pack(): pl.pallas_call(functools.partial(pack_body, rows, bins, first, pieces), i...  7.9 us
    all_to_all x1, starting transfers between devices, on_device(): received = [lax.all_to_all(sent[0], 'pulse', 0, 0, tiled=True)]  6.57 us
  transfers between devices with their start and end apart: 2, of which 2 were waited for; matrix products, arithmetic and copies ran while one was open for 12% of the time, Pallas kernels for 36%

profile of v6, /device:TPU:15, one launch (start us, length us, event | category | flops | bytes accessed | tf_op | source)
XLA Modules:
  0.0 212.5 jit_solution(16739475302072867351)
XLA Ops:
  0.0 4.9 %pack.3 = f32[16,3,2,128,128]{4,3,2,1,0:T(8,128)} custom-call(f32[2,8,128,1024]{3,2,1,0:T(8,128)} %bitcast.2), custom_call_target="tpu_custom_call" | custom-call | bytes 12582912 | tf_op jit(solution)/shard_map/pack/pallas_call | solution.py:139
  5.0 6.6 %all-to-all-start.1 = ((f32[16,3,2,128,128]{4,3,2,1,0:T(8,128)}), f32[16,3,2,128,128]{4,3,2,1,0:T(8,128)}, u32[]{:S(2)}, u32[]{:S(2)}) async-start(f32[16,3,2,128,128]{4,3,2,1,0:T(8,128)} %pack.3), calls=%async_computation.1 | async-start | bytes 12582912 | tf_op jit(solution)/shard_map/all_to_all | solution.py:540
  11.5 3.0 %pack.2 = f32[16,1,2,128,128]{4,3,2,1,0:T(8,128)} custom-call(f32[2,8,128,1024]{3,2,1,0:T(8,128)} %bitcast.3), custom_call_target="tpu_custom_call" | custom-call | bytes 4194304 | tf_op jit(solution)/shard_map/pack/pallas_call | solution.py:139
  14.5 0.8 dynamic-slice_add_fusion
  15.3 0.1 add.112
  15.4 11.4 %fusion.1.shift_ref = s32[16,128,128]{2,1,0:T(8,128)} fusion(s32[16,128]{1,0:T(8,128)S(1)} %get-tuple-element.12, s32[128]{0:T(128)S(1)} %add.112, s32[16,128]{1,0:T(8,128)S(1)} %get-tuple-element.13, s32[128]{0:T(128)S(1)} %get-tuple-element.10, s32[16,128]{1,0:T(8,128)S(1)} %get-tuple-element.11), kind=kLoop, calls=%fused_computation.4 | loop fusion | flops 2097152 | bytes 1074176 | tf_op jit(solution)/shard_map/sub | solution.py:222
  26.8 11.5 %convert_divide_fusion.fraction_ref = f32[16,128,128]{2,1,0:T(8,128)} fusion(f32[128]{0:T(128)S(1)} %get-tuple-element.9, s32[128]{0:T(128)S(1)} %add.112, s32[16,128]{1,0:T(8,128)S(1)} %get-tuple-element.13, s32[128]{0:T(128)S(1)} %get-tuple-element.10, s32[16,128]{1,0:T(8,128)S(1)} %get-tuple-element.11), kind=kLoop, calls=%fused_computation.1 | loop fusion | flops 2883584 | bytes 1066496 | tf_op jit(solution)/shard_map/div | solution.py:221
  38.3 41.7 %weights.1.weight_ref = f32[16,216,8,128]{3,2,1,0:T(8,128)} custom-call(s32[16,128,128]{2,1,0:T(8,128)} %fusion.1.shift_ref, f32[16,128,128]{2,1,0:T(8,128)} %convert_divide_fusion.fraction_ref), custom_call_target="tpu_custom_call" | custom-call | flops 838860800 | bytes 67108864 | tf_op jit(solution)/shard_map/weights/pallas_call | solution.py:225
  79.9 69.0 %all-to-all-done.1.recv_ref = f32[16,3,2,128,128]{4,3,2,1,0:T(8,128)} async-done(((f32[16,3,2,128,128]{4,3,2,1,0:T(8,128)}), f32[16,3,2,128,128]{4,3,2,1,0:T(8,128)}, u32[]{:S(2)}, u32[]{:S(2)}) %all-to-all-start.1) | async-done | bytes 6291488 | tf_op jit(solution)/shard_map/all_to_all | solution.py:540
  148.9 4.9 %all-to-all-start = ((f32[16,1,2,128,128]{4,3,2,1,0:T(8,128)}), f32[16,1,2,128,128]{4,3,2,1,0:T(8,128)S(1)}, u32[]{:S(2)}, u32[]{:S(2)}) async-start(f32[16,1,2,128,128]{4,3,2,1,0:T(8,128)} %pack.2), calls=%async_computation | async-start | bytes 4194304 | tf_op jit(solution)/shard_map/all_to_all | solution.py:543
  153.8 0.7 fusion.10.scale_ref
  154.6 0.0 copy-start
  154.6 32.6 %finish.2.rest_0_ = f32[2,8,64,2048]{3,2,1,0:T(8,128)} custom-call(f32[16,3,2,128,128]{4,3,2,1,0:T(8,128)} %all-to-all-done.1.recv_ref, f32[16,216,8,128]{3,2,1,0:T(8,128)} %weights.1.weight_ref, bf16[16,2,2,256,256]{4,3,2,1,0:T(8,128)(2,1)} %constant.64.clone.turn_ref, f32[1,2048]{1,0:T(1,128)} %fusion.10.scale_ref), custom_call_target="tpu_custom_call" | custom-call | flops 4831838208 | bytes 50331648 | tf_op jit(solution)/shard_map/finish/pallas_call | solution.py:506
  187.2 14.1 %all-to-all-done.recv_ref = f32[16,1,2,128,128]{4,3,2,1,0:T(8,128)S(1)} async-done(((f32[16,1,2,128,128]{4,3,2,1,0:T(8,128)}), f32[16,1,2,128,128]{4,3,2,1,0:T(8,128)S(1)}, u32[]{:S(2)}, u32[]{:S(2)}) %all-to-all-start) | async-done | bytes 2097184 | tf_op jit(solution)/shard_map/all_to_all | solution.py:543
  201.3 0.0 copy-done
  201.3 11.1 %finish.3 = f32[2,8,64,2048]{3,2,1,0:T(8,128)} custom-call(f32[16,1,2,128,128]{4,3,2,1,0:T(8,128)S(1)} %all-to-all-done.recv_ref, f32[16,216,8,128]{3,2,1,0:T(8,128)} %weights.1.weight_ref, bf16[16,2,2,256,256]{4,3,2,1,0:T(8,128)(2,1)} %constant.64.clone.turn_ref, f32[1,2048]{1,0:T(1,128)S(1)} %copy-done, ...), custom_call_target="tpu_custom_call", output_to_operand_aliasing={{}: (4, {})} | custom-call | flops 1610612736 | bytes 41943040 | tf_op jit(solution)/shard_map/finish/pallas_call | solution.py:506
  (4 shorter events, 0.0 us)
Async XLA Ops:
  5.0 144.0 %all-to-all-start.1 = ((f32[16,3,2,128,128]{4,3,2,1,0:T(8,128)}), f32[16,3,2,128,128]{4,3,2,1,0:T(8,128)}, u32[]{:S(2)}, u32[]{:S(2)}) async-start(f32[16,3,2,128,128]{4,3,2,1,0:T(8,128)} %pack.3), calls=%async_computation.1 | async-start | bytes 12582912 | tf_op jit(solution)/shard_map/all_to_all | solution.py:540
  148.9 52.3 %all-to-all-start = ((f32[16,1,2,128,128]{4,3,2,1,0:T(8,128)}), f32[16,1,2,128,128]{4,3,2,1,0:T(8,128)S(1)}, u32[]{:S(2)}, u32[]{:S(2)}) async-start(f32[16,1,2,128,128]{4,3,2,1,0:T(8,128)} %pack.2), calls=%async_computation | async-start | bytes 4194304 | tf_op jit(solution)/shard_map/all_to_all | solution.py:543
  154.6 46.7 %copy-start = (f32[1,2048]{1,0:T(1,128)S(1)}, f32[1,2048]{1,0:T(1,128)}, u32[]{:S(2)}) copy-start(f32[1,2048]{1,0:T(1,128)} %fusion.10.scale_ref) | copy-start | bytes 24580

commit v7 on v6

--- a/solution.py
+++ b/solution.py
@@ -403,7 +403,7 @@
             if row >= CUTS:
                 depart(row - CUTS).wait()
 
-            @pl.loop(0, bins // 8, unroll=2)
+            @pl.loop(0, bins // 8, unroll=4)
             def _(group):
                 here = pl.ds(pl.multiple_of(group * 8, 8), 8)
 
@@ -464,7 +464,7 @@
 
     if close:
         begin()
-        pl.loop(0, MINOR)(step)
+        pl.loop(0, MINOR, unroll=2)(step)
         end_close()
     else:
         now = pl.program_id(0)

time: 213 us -> 213 us (level)
  no operation moved by 1% of the time
where the time goes in v7:
time: 213 us; the launch traced here: 212 us
  Pallas kernels  93.2 us (44%)
  waiting for transfers between devices  83.1 us (39%)
  other arithmetic  24.4 us (11%)
  starting transfers between devices  11.5 us (5%)
    all_to_all x1, waiting for transfers between devices, on_device(): received = [lax.all_to_all(sent[0], 'pulse', 0, 0, tiled=True)]  69 us
    pallas_call x2, Pallas kernels, finish(): pl.pallas_call(functools.partial(main_body, first, count, rows, bins, bas...  43.6 us
    pallas_call x1, Pallas kernels, weights(): pl.pallas_call(functools.partial(weight_body, bins), grid=(MINOR,), in_sp...  41.7 us
    all_to_all x1, waiting for transfers between devices, on_device(): received.append(lax.all_to_all(later, 'pulse', 0, 0, tiled=True))  14.1 us
    div x1, other arithmetic, weights(): (numerator - cell_floor * denominator).astype(jnp.float32)  11.5 us
    sub x1, other arithmetic, weights(): shift = cell_floor - 2 * slow  11.4 us
    pallas_call x2, Pallas kernels, pack(): pl.pallas_call(functools.partial(pack_body, rows, bins, first, pieces), i...  7.9 us
    all_to_all x1, starting transfers between devices, on_device(): received = [lax.all_to_all(sent[0], 'pulse', 0, 0, tiled=True)]  6.57 us
  transfers between devices with their start and end apart: 2, of which 2 were waited for; matrix products, arithmetic and copies ran while one was open for 12% of the time, Pallas kernels for 36%

profile of v7, /device:TPU:15, one launch (start us, length us, event | category | flops | bytes accessed | tf_op | source)
XLA Modules:
  0.0 212.4 jit_solution(14553010363534852234)
XLA Ops:
  0.0 4.9 %pack.3 = f32[16,3,2,128,128]{4,3,2,1,0:T(8,128)} custom-call(f32[2,8,128,1024]{3,2,1,0:T(8,128)} %bitcast.2), custom_call_target="tpu_custom_call" | custom-call | bytes 12582912 | tf_op jit(solution)/shard_map/pack/pallas_call | solution.py:139
  5.0 6.6 %all-to-all-start.1 = ((f32[16,3,2,128,128]{4,3,2,1,0:T(8,128)}), f32[16,3,2,128,128]{4,3,2,1,0:T(8,128)}, u32[]{:S(2)}, u32[]{:S(2)}) async-start(f32[16,3,2,128,128]{4,3,2,1,0:T(8,128)} %pack.3), calls=%async_computation.1 | async-start | bytes 12582912 | tf_op jit(solution)/shard_map/all_to_all | solution.py:540
  11.5 3.0 %pack.2 = f32[16,1,2,128,128]{4,3,2,1,0:T(8,128)} custom-call(f32[2,8,128,1024]{3,2,1,0:T(8,128)} %bitcast.3), custom_call_target="tpu_custom_call" | custom-call | bytes 4194304 | tf_op jit(solution)/shard_map/pack/pallas_call | solution.py:139
  14.5 0.8 dynamic-slice_add_fusion
  15.3 0.1 add.112
  15.4 11.4 %fusion.1.shift_ref = s32[16,128,128]{2,1,0:T(8,128)} fusion(s32[16,128]{1,0:T(8,128)S(1)} %get-tuple-element.12, s32[128]{0:T(128)S(1)} %add.112, s32[16,128]{1,0:T(8,128)S(1)} %get-tuple-element.13, s32[128]{0:T(128)S(1)} %get-tuple-element.10, s32[16,128]{1,0:T(8,128)S(1)} %get-tuple-element.11), kind=kLoop, calls=%fused_computation.4 | loop fusion | flops 2097152 | bytes 1074176 | tf_op jit(solution)/shard_map/sub | solution.py:222
  26.8 11.5 %convert_divide_fusion.fraction_ref = f32[16,128,128]{2,1,0:T(8,128)} fusion(f32[128]{0:T(128)S(1)} %get-tuple-element.9, s32[128]{0:T(128)S(1)} %add.112, s32[16,128]{1,0:T(8,128)S(1)} %get-tuple-element.13, s32[128]{0:T(128)S(1)} %get-tuple-element.10, s32[16,128]{1,0:T(8,128)S(1)} %get-tuple-element.11), kind=kLoop, calls=%fused_computation.1 | loop fusion | flops 2883584 | bytes 1066496 | tf_op jit(solution)/shard_map/div | solution.py:221
  38.3 41.7 %weights.1.weight_ref = f32[16,216,8,128]{3,2,1,0:T(8,128)} custom-call(s32[16,128,128]{2,1,0:T(8,128)} %fusion.1.shift_ref, f32[16,128,128]{2,1,0:T(8,128)} %convert_divide_fusion.fraction_ref), custom_call_target="tpu_custom_call" | custom-call | flops 838860800 | bytes 67108864 | tf_op jit(solution)/shard_map/weights/pallas_call | solution.py:225
  79.9 69.0 %all-to-all-done.1.recv_ref = f32[16,3,2,128,128]{4,3,2,1,0:T(8,128)} async-done(((f32[16,3,2,128,128]{4,3,2,1,0:T(8,128)}), f32[16,3,2,128,128]{4,3,2,1,0:T(8,128)}, u32[]{:S(2)}, u32[]{:S(2)}) %all-to-all-start.1) | async-done | bytes 6291488 | tf_op jit(solution)/shard_map/all_to_all | solution.py:540
  148.9 4.9 %all-to-all-start = ((f32[16,1,2,128,128]{4,3,2,1,0:T(8,128)}), f32[16,1,2,128,128]{4,3,2,1,0:T(8,128)S(1)}, u32[]{:S(2)}, u32[]{:S(2)}) async-start(f32[16,1,2,128,128]{4,3,2,1,0:T(8,128)} %pack.2), calls=%async_computation | async-start | bytes 4194304 | tf_op jit(solution)/shard_map/all_to_all | solution.py:543
  153.8 0.7 fusion.10.scale_ref
  154.6 0.0 copy-start
  154.6 32.6 %finish.2.rest_0_ = f32[2,8,64,2048]{3,2,1,0:T(8,128)} custom-call(f32[16,3,2,128,128]{4,3,2,1,0:T(8,128)} %all-to-all-done.1.recv_ref, f32[16,216,8,128]{3,2,1,0:T(8,128)} %weights.1.weight_ref, bf16[16,2,2,256,256]{4,3,2,1,0:T(8,128)(2,1)} %constant.64.clone.turn_ref, f32[1,2048]{1,0:T(1,128)} %fusion.10.scale_ref), custom_call_target="tpu_custom_call" | custom-call | flops 4831838208 | bytes 50331648 | tf_op jit(solution)/shard_map/finish/pallas_call | solution.py:506
  187.2 14.1 %all-to-all-done.recv_ref = f32[16,1,2,128,128]{4,3,2,1,0:T(8,128)S(1)} async-done(((f32[16,1,2,128,128]{4,3,2,1,0:T(8,128)}), f32[16,1,2,128,128]{4,3,2,1,0:T(8,128)S(1)}, u32[]{:S(2)}, u32[]{:S(2)}) %all-to-all-start) | async-done | bytes 2097184 | tf_op jit(solution)/shard_map/all_to_all | solution.py:543
  201.3 0.0 copy-done
  201.3 11.0 %finish.3 = f32[2,8,64,2048]{3,2,1,0:T(8,128)} custom-call(f32[16,1,2,128,128]{4,3,2,1,0:T(8,128)S(1)} %all-to-all-done.recv_ref, f32[16,216,8,128]{3,2,1,0:T(8,128)} %weights.1.weight_ref, bf16[16,2,2,256,256]{4,3,2,1,0:T(8,128)(2,1)} %constant.64.clone.turn_ref, f32[1,2048]{1,0:T(1,128)S(1)} %copy-done, ...), custom_call_target="tpu_custom_call", output_to_operand_aliasing={{}: (4, {})} | custom-call | flops 1610612736 | bytes 41943040 | tf_op jit(solution)/shard_map/finish/pallas_call | solution.py:506
  (4 shorter events, 0.0 us)
Async XLA Ops:
  5.0 144.0 %all-to-all-start.1 = ((f32[16,3,2,128,128]{4,3,2,1,0:T(8,128)}), f32[16,3,2,128,128]{4,3,2,1,0:T(8,128)}, u32[]{:S(2)}, u32[]{:S(2)}) async-start(f32[16,3,2,128,128]{4,3,2,1,0:T(8,128)} %pack.3), calls=%async_computation.1 | async-start | bytes 12582912 | tf_op jit(solution)/shard_map/all_to_all | solution.py:540
  148.9 52.3 %all-to-all-start = ((f32[16,1,2,128,128]{4,3,2,1,0:T(8,128)}), f32[16,1,2,128,128]{4,3,2,1,0:T(8,128)S(1)}, u32[]{:S(2)}, u32[]{:S(2)}) async-start(f32[16,1,2,128,128]{4,3,2,1,0:T(8,128)} %pack.2), calls=%async_computation | async-start | bytes 4194304 | tf_op jit(solution)/shard_map/all_to_all | solution.py:543
  154.6 46.7 %copy-start = (f32[1,2048]{1,0:T(1,128)S(1)}, f32[1,2048]{1,0:T(1,128)}, u32[]{:S(2)}) copy-start(f32[1,2048]{1,0:T(1,128)} %fusion.10.scale_ref) | copy-start | bytes 24580
